TPU v7x, 32 devices: a whole 2x2x4 slice. The times are simulated.
32 devices in a mesh: seq: 8 (over y, x, core), tp: 4 (over z).
Axes of the slice: x: 2, y: 2, z: 4, core: 2. Of those that a mesh axis runs over, the one named last changes fastest.
Arguments:
- hidden: bfloat16 [6144, 8192], P('seq', 'tp'), may hold values from -6 to 6
- cotangent: bfloat16 [6144, 8192], P('seq', 'tp'), may hold values from -0.59765625 to 0.59765625
- router_gate: bfloat16 [6144], P('seq'), may hold values from 0.25 to 1
- recursion_depth: int32 [6144], P('seq'), may hold values from 1 to 4
- live_counts: int32 [8], replicated, may hold values from 0 to 768, as said below
- out_weight: bfloat16 [8192, 8192], P(None, 'tp'), may hold values from -0.0625 to 0.0625
- adapter_down: bfloat16 [8192, 1024], P('tp', 'seq'), may hold values from -0.0625 to 0.0625
- adapter_up: bfloat16 [1024, 8192], P('seq', 'tp'), may hold values from -0.375 to 0.375
Outputs:
- hidden_grad: float32 [6144, 8192], P('seq', 'tp')
- gate_grad: float32 [6144], P('seq')
- weight_grad: float32 [8192, 8192], P('seq', 'tp')
- down_grad: float32 [1024, 8192], P('seq', 'tp')
- up_grad: float32 [1024, 8192], P('seq', 'tp')
Inputs may be any that keep to these rules, and one draw needn't show every extreme that they name: `live_counts`: each entry is a multiple of 128; the entries sum to 3072; the largest entry equals 768. Rows at or past an index's count are not live.
All inputs are finite; a program needn't handle non-finite values.
Results may differ from a plain program's by a relative error of at most 0.0055.
Values may be sent and summed in bfloat16 or wider, within the bound.
No kernel may reach another device: no remote copies, remote signals or barrier semaphores. Data moves between devices by JAX's collectives and lax.ppermute only.
A program may use at most 256 MiB of HBM per device.

v0:
```python
import jax
import jax.numpy as jnp
from jax import lax
from jax.sharding import PartitionSpec as P

NREC = 4
BAL = 384


adapter_scale = 0.5
contract_rows = (((0,), (0,)), ((), ()))
contract_last = (((1,), (1,)), ((), ()))


def select_block(wide_values, selector):
    row_total = wide_values.shape[0]
    return jnp.sum(
        wide_values.reshape(row_total, selector.shape[1], -1) * selector[:, :, None], axis=1
    )


def spread_block(values, selector):
    return (selector[:, :, None] * values[:, None, :]).reshape(values.shape[0], -1)


def local(
    hidden,
    cotangent,
    router_gate,
    recursion_depth,
    live_counts,
    out_weight,
    adapter_down,
    adapter_up,
):
    shards = lax.axis_size("seq")
    slot_count = hidden.shape[0]
    width_local = hidden.shape[1]
    per_pair = slot_count // shards
    shares = live_counts // shards
    finish = jnp.cumsum(shares)
    starts_at = finish - shares
    shard_ids = jnp.arange(shards, dtype=jnp.int32)
    adapters_down, adapters_up = (
        lax.all_gather(adapter_down, "seq", axis=1, tiled=True),
        lax.all_gather(adapter_up, "seq", axis=0, tiled=True),
    )
    rank_slots = jnp.arange(BAL, dtype=jnp.int32)
    source = jnp.sum((finish[None, :] <= rank_slots[:, None]).astype(jnp.int32), axis=1)
    begin_at = jnp.sum(
        jnp.where(source[:, None] == shard_ids[None, :], starts_at[None, :], 0), axis=1
    )
    pick_rows = (rank_slots - begin_at) * shards + source
    arrived = (
        lax.all_to_all(
            hidden.reshape(per_pair, shards, width_local),
            "seq",
            split_axis=1,
            concat_axis=1,
            tiled=True,
        ),
        lax.all_to_all(
            cotangent.reshape(per_pair, shards, width_local),
            "seq",
            split_axis=1,
            concat_axis=1,
            tiled=True,
        ),
        lax.all_to_all(
            router_gate.reshape(per_pair, shards), "seq", split_axis=1, concat_axis=1, tiled=True
        ),
        lax.all_to_all(
            recursion_depth.astype(jnp.bfloat16).reshape(per_pair, shards),
            "seq",
            split_axis=1,
            concat_axis=1,
            tiled=True,
        ),
    )
    rows_h = jnp.take(arrived[0].reshape(slot_count, width_local), pick_rows, axis=0)
    rows_dy = jnp.take(arrived[1].reshape(slot_count, width_local), pick_rows, axis=0)
    gate_rows = jnp.take(arrived[2].reshape(slot_count), pick_rows).astype(jnp.float32)
    depths = jnp.take(arrived[3].reshape(slot_count), pick_rows).astype(jnp.float32)
    live_mask = jnp.ones((BAL,), dtype=bool)
    levels = jnp.arange(1, NREC + 1, dtype=jnp.float32)
    selector = (depths[:, None] == levels[None, :]).astype(jnp.float32)
    full_dy = lax.all_gather(rows_dy, "tp", axis=1, tiled=True)
    gated_dy = (gate_rows[:, None] * full_dy).astype(jnp.bfloat16)
    down_part = jnp.dot(rows_h, adapters_down, preferred_element_type=jnp.float32)
    up_part = lax.dot_general(
        rows_dy, adapters_up, contract_last, preferred_element_type=jnp.float32
    )
    down_proj, up_summed = lax.psum(
        (select_block(down_part, selector), select_block(up_part, selector)), "tp"
    )
    up_back = adapter_scale * up_summed
    wide_back = spread_block(up_back, selector)
    wide_down = spread_block(down_proj, selector)
    pre_grad = jnp.dot(full_dy, out_weight, preferred_element_type=jnp.float32)
    pre_grad = pre_grad + lax.dot_general(
        wide_back.astype(jnp.bfloat16),
        adapters_down,
        contract_last,
        preferred_element_type=jnp.float32,
    )
    row_grad = gate_rows[:, None] * pre_grad
    gate_part = jnp.sum(rows_h.astype(jnp.float32) * pre_grad, axis=1)
    gate_total = lax.psum(gate_part, "tp")
    gate_row = jnp.where(live_mask, gate_total, 0.0)
    back_gated = (gate_rows[:, None] * wide_back).astype(jnp.bfloat16)
    down_gated = (gate_rows[:, None] * adapter_scale * wide_down).astype(jnp.bfloat16)
    down_local = lax.dot_general(
        back_gated, rows_h, contract_rows, preferred_element_type=jnp.float32
    )
    up_local = lax.dot_general(
        down_gated, rows_dy, contract_rows, preferred_element_type=jnp.float32
    )
    down_grad, up_grad = (
        lax.psum_scatter(down_local, "seq", scatter_dimension=0, tiled=True),
        lax.psum_scatter(up_local, "seq", scatter_dimension=0, tiled=True),
    )
    weight_grad = lax.psum_scatter(
        lax.dot_general(gated_dy, rows_h, contract_rows, preferred_element_type=jnp.float32),
        "seq",
        scatter_dimension=0,
        tiled=True,
    )
    position = jnp.arange(slot_count, dtype=jnp.int32)
    within = position // shards
    owner_shard = position % shards
    owner_pick = owner_shard[:, None] == shard_ids[None, :]
    alive_mask = within < jnp.sum(jnp.where(owner_pick, shares[None, :], 0), axis=1)
    back_rows = jnp.where(
        alive_mask, jnp.sum(jnp.where(owner_pick, starts_at[None, :], 0), axis=1) + within, 0
    )
    grad_slots = jnp.where(alive_mask[:, None], jnp.take(row_grad, back_rows, axis=0), 0.0)
    gate_slots = jnp.where(alive_mask, jnp.take(gate_row, back_rows), 0.0)
    returned = (
        lax.all_to_all(
            grad_slots.reshape(per_pair, shards, width_local),
            "seq",
            split_axis=1,
            concat_axis=1,
            tiled=True,
        ),
        lax.all_to_all(
            gate_slots.reshape(per_pair, shards), "seq", split_axis=1, concat_axis=1, tiled=True
        ),
    )
    hidden_grad = returned[0].reshape(slot_count, width_local)
    gate_grad = returned[1].reshape(slot_count)
    return (hidden_grad, gate_grad, weight_grad, down_grad, up_grad)


def solution(mesh):
    in_specs = (
        P("seq", "tp"),
        P("seq", "tp"),
        P("seq"),
        P("seq"),
        P(),
        P(None, "tp"),
        P("tp", "seq"),
        P("seq", "tp"),
    )
    out_specs = (P("seq", "tp"), P("seq"), P("seq", "tp"), P("seq", "tp"), P("seq", "tp"))
    return jax.shard_map(local, mesh=mesh, in_specs=in_specs, out_specs=out_specs, check_vma=False)
```

profile of v0, /device:TPU:0, one launch (start us, length us, event | category | flops | bytes accessed | tf_op | source)
XLA Modules:
  0.0 932.0 jit_solution(17807375785075924170)
XLA Ops:
  10.1 5.2 all-to-all-start.2
  16.8 3.1 all-to-all-done.2
  19.9 3.3 all-to-all-start
  23.2 5.3 copy.63
  28.5 4.1 all-to-all-start.4
  32.6 5.4 copy.56
  38.0 43.7 %all-to-all-done.4 = bf16[96,8,2048]{2,0,1:T(8,128)(2,1)S(1)} async-done(((bf16[96,8,2048]{2,0,1:T(8,128)(2,1)}), bf16[96,8,2048]{2,0,1:T(8,128)(2,1)S(1)}, u32[]{:S(2)}, u32[]{:S(2)}) %all-to-all-start.4) | async-done | bytes 3145760 | tf_op jit(solution)/shard_map/all_to_all | solution.py:55
  83.4 4.5 all-to-all-start.1
  94.8 3.6 copy.76
  98.5 3.1 gather_fusion.5
  101.6 40.1 %all-to-all-done.1 = bf16[96,8,2048]{2,0,1:T(8,128)(2,1)} async-done(((bf16[96,8,2048]{2,0,1:T(8,128)(2,1)}), bf16[96,8,2048]{2,0,1:T(8,128)(2,1)}, u32[]{:S(2)}, u32[]{:S(2)}) %all-to-all-start.1) | async-done | bytes 3145760 | tf_op jit(solution)/shard_map/all_to_all | solution.py:62
  141.7 3.6 copy.77
  145.3 3.1 gather_fusion.3
  150.3 5.6 fusion.17
  158.8 5.2 fusion.20
  167.0 4.7 multiply_reduce_fusion.1
  172.3 42.7 %all-reduce.3.cloned.1.call-done = (f32[384,256]{1,0:T(8,128)}, f32[384,256]{1,0:T(8,128)}) async-done(((f32[384,256]{1,0:T(8,128)}, f32[384,256]{1,0:T(8,128)}), (f32[384,256]{1,0:T(8,128)}, f32[384,256]{1,0:T(8,128)})) %all-reduce.3.cloned.1.call-update) | async-done | bytes 786448 | tf_op jit(solution)/shard_map/psum | solution.py:93
  219.2 6.3 fusion.4
  227.2 5.8 fusion.3
  233.1 98.6 %all-gather.4.cloned.1.call-done = bf16[384,8192]{1,0:T(8,128)(2,1)} async-done(((bf16[384,2048]{1,0:T(8,128)(2,1)}), bf16[384,8192]{1,0:T(8,128)(2,1)}) %all-gather.4.cloned.1.call-update) | async-done | bytes 6291472 | tf_op jit(solution)/shard_map/all_gather | solution.py:87
  331.6 33.7 %fusion = f32[8192,2048]{1,0:T(8,128)} fusion(bf16[384,8192]{1,0:T(8,128)(2,1)} %all-gather.4.cloned.1.call-done, f32[384]{0:T(512)S(1)} %get-tuple-element.21, bf16[384,2048]{1,0:T(8,128)(2,1)S(1)} %copy-done, pred[384]{0:T(512)(128)(4,1)S(1)} %get-tuple-element.14), kind=kOutput, calls=%fused_computation.7 | convolution fusion | flops 12895125504 | bytes 74975104 | tf_op jit(solution)/shard_map/dot_general | solution.py:123
  366.0 22.8 %fusion.19 = f32[384,2048]{1,0:T(8,128)} fusion(bf16[384,8192]{1,0:T(8,128)(2,1)} %all-gather.4.cloned.1.call-done, bf16[8192,2048]{1,0:T(8,128)(2,1)} %param.17), kind=kOutput, calls=%fused_computation.84 | convolution fusion | flops 12884901888 | bytes 42991616 | tf_op jit(solution)/shard_map/dot_general | solution.py:99
  388.9 6.1 multiply_reduce_fusion
  395.0 8.4 psum.22
  403.4 5.0 gather_fusion.1
  409.2 4.1 all-to-all-start.5
  413.3 4.9 gather_fusion
  418.2 9.5 %fusion.1 = f32[96,8,2048]{2,0,1:T(8,128)} fusion(f32[96,8,2048]{2,1,0:T(8,128)} %bitcast.35, pred[96,8]{0,1:T(8,128)(4,1)S(1)} %get-tuple-element.15, pred[96,8]{0,1:T(8,128)(4,1)S(1)} %get-tuple-element.16), kind=kLoop, calls=%fused_computation.10 | loop fusion | flops 3145728 | bytes 12584448 | tf_op jit(solution)/shard_map/jit(_where)/select_n | solution.py:136
  427.7 4.7 all-to-all-start.3
  433.3 97.2 %all-to-all-done.3 = f32[96,8,2048]{2,0,1:T(8,128)} async-done(((f32[96,8,2048]{2,0,1:T(8,128)}), f32[96,8,2048]{2,0,1:T(8,128)}, u32[]{:S(2)}, u32[]{:S(2)}) %all-to-all-start.3) | async-done | bytes 6291488 | tf_op jit(solution)/shard_map/all_to_all | solution.py:139
  530.5 9.1 copy.75
  539.6 385.3 %reduce-scatter.4.cloned.1.call-done = f32[1024,2048]{1,0:T(8,128)} async-done(((f32[8192,2048]{1,0:T(8,128)}), f32[1024,2048]{1,0:T(8,128)}) %reduce-scatter.4.cloned.1.call-update) | async-done | bytes 8388624 | tf_op jit(solution)/shard_map/reduce_scatter | solution.py:122
  (85 shorter events, 29.3 us)
Async XLA Ops:
  7.2 143.1 %all-gather.8.cloned.1.call-start = ((), (), s32[]{:S(2)}) async-start(), calls=%async_computation.11 | async-start | bytes 4718592 | tf_op jit(solution)/shard_map/all_gather | solution.py:45
  7.9 150.9 %all-gather.6.cloned.1.call-start = ((), (), s32[]{:S(2)}) async-start(), calls=%async_computation.10 | async-start | bytes 4718592 | tf_op jit(solution)/shard_map/all_gather | solution.py:46
  10.1 9.8 %all-to-all-start.2 = ((bf16[96,8,1]{0,2,1:T(2,128)(2,1)}), bf16[96,8,1]{0,2,1:T(2,128)(2,1)S(1)}, u32[]{:S(2)}, u32[]{:S(2)}) async-start(bf16[96,8,1]{0,2,1:T(2,128)(2,1)} %copy.58), calls=%async_computation.2 | async-start | bytes 8192 | tf_op jit(solution)/shard_map/all_to_all | solution.py:72
  19.9 8.6 all-to-all-start
  28.5 53.2 %all-to-all-start.4 = ((bf16[96,8,2048]{2,0,1:T(8,128)(2,1)}), bf16[96,8,2048]{2,0,1:T(8,128)(2,1)S(1)}, u32[]{:S(2)}, u32[]{:S(2)}) async-start(bf16[96,8,2048]{2,0,1:T(8,128)(2,1)} %copy.63), calls=%async_computation.4 | async-start | bytes 6291456 | tf_op jit(solution)/shard_map/all_to_all | solution.py:55
  38.0 49.9 %copy-start.8 = (s32[8]{0:T(128)S(1)}, s32[8]{0:T(128)}, u32[]{:S(2)}) copy-start(s32[8]{0:T(128)} %param.16) | copy-start | bytes 100
  81.7 1.7 copy-start.6
  83.4 58.3 %all-to-all-start.1 = ((bf16[96,8,2048]{2,0,1:T(8,128)(2,1)}), bf16[96,8,2048]{2,0,1:T(8,128)(2,1)}, u32[]{:S(2)}, u32[]{:S(2)}) async-start(bf16[96,8,2048]{2,0,1:T(8,128)(2,1)} %copy.56), calls=%async_computation.1 | async-start | bytes 6291456 | tf_op jit(solution)/shard_map/all_to_all | solution.py:62
  87.9 127.1 %all-reduce.3.cloned.1.call-start = ((), (), s32[]{:S(2)}) async-start(), calls=%async_computation.15 | async-start | bytes 1572864 | tf_op jit(solution)/shard_map/psum | solution.py:93
  148.5 1.9 copy-start
  150.2 8.7 copy-start.4
  164.0 3.0 copy-start.7
  171.7 160.0 %all-gather.4.cloned.1.call-start = ((), (), s32[]{:S(2)}) async-start(), calls=%async_computation.9 | async-start | bytes 7864320 | tf_op jit(solution)/shard_map/all_gather | solution.py:87
  172.2 367.4 %reduce-scatter.8.cloned.1.call-start = ((), (), s32[]{:S(2)}) async-start(), calls=%async_computation.14 | async-start | bytes 9437184 | tf_op jit(solution)/shard_map/reduce_scatter | solution.py:120
  217.8 1.4 copy-start.5
  225.5 314.1 %reduce-scatter.6.cloned.1.call-start = ((), (), s32[]{:S(2)}) async-start(), calls=%async_computation.13 | async-start | bytes 9437184 | tf_op jit(solution)/shard_map/reduce_scatter | solution.py:119
  225.9 1.3 copy-start.2
  233.0 691.9 %reduce-scatter.4.cloned.1.call-start = ((), (), s32[]{:S(2)}) async-start(), calls=%async_computation.12 | async-start | bytes 75497472 | tf_op jit(solution)/shard_map/reduce_scatter | solution.py:122
  366.0 22.9 %copy-start.1 = (bf16[384,2048]{1,0:T(8,128)(2,1)S(1)}, bf16[384,2048]{1,0:T(8,128)(2,1)}, u32[]{:S(2)}) copy-start(bf16[384,2048]{1,0:T(8,128)(2,1)} %gather_fusion.5) | copy-start | bytes 4718596
  366.0 22.9 %copy-start.3 = (f32[48,8,4,256]{3,1,2,0:T(8,128)S(1)}, f32[48,8,4,256]{3,1,2,0:T(8,128)}, u32[]{:S(2)}) copy-start(f32[48,8,4,256]{3,1,2,0:T(8,128)} %copy-done.2) | copy-start | bytes 4718596
  409.2 18.5 %all-to-all-start.5 = ((f32[96,8,1]{0,2,1:T(1,128)}), f32[96,8,1]{0,2,1:T(1,128)S(1)}, u32[]{:S(2)}, u32[]{:S(2)}) async-start(f32[96,8,1]{0,2,1:T(1,128)} %copy.65), calls=%async_computation.5 | async-start | bytes 8192 | tf_op jit(solution)/shard_map/all_to_all | solution.py:146
  427.7 102.7 %all-to-all-start.3 = ((f32[96,8,2048]{2,0,1:T(8,128)}), f32[96,8,2048]{2,0,1:T(8,128)}, u32[]{:S(2)}, u32[]{:S(2)}) async-start(f32[96,8,2048]{2,0,1:T(8,128)} %fusion.1), calls=%async_computation.3 | async-start | bytes 12582912 | tf_op jit(solution)/shard_map/all_to_all | solution.py:139
Sparse Core Ops, SparseCore 0:
  9.9 59.7 all-gather.7
  71.6 70.0 all-gather.5
  171.8 43.1 all-reduce.2
  217.0 114.5 all-gather.3
  335.5 69.4 reduce-scatter.7
  409.3 129.7 reduce-scatter.5
  543.3 381.6 reduce-scatter.3
where the time goes:
time: 943 us; the launch traced here: 932 us
  waiting for transfers between devices  713 us (76%)
  matrix products  85.5 us (9%)
  local copies, waits for them, and re-layouts  64.4 us (7%)
  starting transfers between devices  26.2 us (3%)
  other arithmetic  20 us (2%)
  between operations  14.6 us (2%)
    reduce_scatter x1, waiting for transfers between devices, local(): lax.psum_scatter(lax.dot_general(gated_dy, rows_h, contract_rows, preferr...  385 us
    all_gather x1, waiting for transfers between devices, local(): full_dy = lax.all_gather(rows_dy, 'tp', axis=1, tiled=True)  98.6 us
    all_to_all x1, waiting for transfers between devices, local(): lax.all_to_all(grad_slots.reshape(per_pair, shards, width_local), 'seq',...  97.2 us
    all_to_all x1, waiting for transfers between devices, local(): lax.all_to_all(hidden.reshape(per_pair, shards, width_local), 'seq', spli...  43.7 us
    psum x1, waiting for transfers between devices, local(): lax.psum((select_block(down_part, selector), select_block(up_part, select...  42.7 us
    all_to_all x1, waiting for transfers between devices, local(): lax.all_to_all(cotangent.reshape(per_pair, shards, width_local), 'seq', s...  40.1 us
    dot_general x1, matrix products, local(): lax.dot_general(gated_dy, rows_h, contract_rows, preferred_element_type=j...  33.7 us
    dot_general x1, matrix products, local(): pre_grad = jnp.dot(full_dy, out_weight, preferred_element_type=jnp.float32)  22.8 us
  transfers between devices with their start and end apart: 13, of which 7 were waited for; matrix products, arithmetic and copies ran while one was open for 16% of the time, Pallas kernels for 0%

commit v1 on v0

v1 whole, which is shorter than its diff:
```python
import jax
import jax.numpy as jnp
from jax import lax
from jax.sharding import PartitionSpec as P

NREC = 4
CHUNKS = 4
adapter_scale = 0.5
contract_rows = (((0,), (0,)), ((), ()))
contract_last = (((1,), (1,)), ((), ()))
f32 = jnp.float32
bf16 = jnp.bfloat16


def dot_rows(a, b):
    return lax.dot_general(a, b, contract_rows, preferred_element_type=f32)


def flip(value, bit):
    size = lax.axis_size("seq")
    return lax.ppermute(value, "seq", [(i, i ^ (1 << bit)) for i in range(size)])


def after(value, earlier):
    return lax.optimization_barrier((value, earlier))[0]


def masks_of(bits):
    masks = [0]
    for bit in bits:
        masks = masks + [m | (1 << bit) for m in masks]
    return masks


def gather_seq(block, bits):
    size, me = lax.axis_size("seq"), lax.axis_index("seq")
    have = block[None]
    for bit in bits:
        have = jnp.concatenate([have, flip(have, bit)], axis=0)
    place = [0] * size
    for at, mask in enumerate(masks_of(bits)):
        place[mask] = at
    order = jnp.take(jnp.array(place, jnp.int32), me ^ jnp.arange(size, dtype=jnp.int32))
    have = jnp.take(have, order, axis=0, mode="clip")
    return have.reshape(size * block.shape[0], block.shape[1])


def gather_line(own, earlier):
    size, me = lax.axis_size("tp"), lax.axis_index("tp")
    if earlier is not None:
        own = after(own, earlier)
    ups, downs = [own], [own]
    for k in range(1, size):
        ups.append(lax.ppermute(ups[-1], "tp", [(i, i + 1) for i in range(k - 1, size - 1)]))
        downs.append(lax.ppermute(downs[-1], "tp", [(i, i - 1) for i in range(1, size - k + 1)]))
    line = jnp.concatenate(ups[:0:-1] + [own] + downs[1:], axis=1)
    width = own.shape[1]
    return lax.dynamic_slice_in_dim(line, (size - 1 - me) * width, size * width, axis=1), (ups[1], downs[1])


def sum_line(part):
    size = lax.axis_size("tp")
    below = above = jnp.zeros_like(part)
    for k in range(1, size):
        below = below + lax.ppermute((part + below).astype(bf16), "tp", [(k - 1, k)]).astype(f32)
        above = above + lax.ppermute((part + above).astype(bf16), "tp", [(size - k, size - k - 1)]).astype(f32)
    return part + below + above


def local(
    hidden,
    cotangent,
    router_gate,
    recursion_depth,
    live_counts,
    out_weight,
    adapter_down,
    adapter_up,
):
    shards, planes = lax.axis_size("seq"), lax.axis_size("tp")
    me = lax.axis_index("seq")
    core, chip = me & 1, me >> 1
    chips = shards // 2
    chip_bits = list(range(1, shards.bit_length() - 1))
    rows, width = hidden.shape
    own_outs = width * planes // shards
    per_block = width // own_outs
    cut = own_outs // CHUNKS
    rank_rows = adapter_up.shape[0]
    rank = rank_rows * shards // NREC

    live = jnp.arange(rows, dtype=jnp.int32) < lax.dynamic_index_in_dim(live_counts, me, 0, False)
    dy = jnp.where(live[:, None], cotangent, jnp.zeros((), bf16))
    small = jnp.stack([router_gate, recursion_depth.astype(bf16)])
    small_both = jnp.concatenate([small, flip(small, 0)], axis=1)
    gate_both, depth_both = small_both[0].astype(f32), small_both[1].astype(f32)
    gate, depth = router_gate.astype(f32), recursion_depth.astype(f32)

    dy_cut = dy.reshape(rows, per_block, CHUNKS, cut)
    gathered, earlier = [], None
    for j in range(CHUNKS):
        piece = dy_cut[:, :, j].reshape(rows, per_block * cut)
        whole, earlier = gather_line(piece, earlier)
        gathered.append(whole)

    hidden_both = jnp.concatenate([hidden, flip(hidden, 0)], axis=0)
    dy_both = jnp.concatenate([dy, flip(dy, 0)], axis=0)
    gated_hidden = (gate_both[:, None] * hidden_both.astype(f32)).astype(bf16)

    downs_t = gather_seq(adapter_down.T, chip_bits + [0])
    ups = gather_seq(adapter_up, chip_bits[::-1] + [0])

    def select(wide):
        return sum(
            jnp.where((depth == d + 1)[:, None], wide[:, d * rank : (d + 1) * rank], 0.0)
            for d in range(NREC)
        )

    down_part = select(lax.dot_general(hidden, downs_t, contract_last, preferred_element_type=f32))
    up_part = select(lax.dot_general(dy, ups, contract_last, preferred_element_type=f32))
    summed = sum_line(jnp.concatenate([down_part, up_part], axis=1))
    down, up = summed[:, :rank], adapter_scale * summed[:, rank:]
    wide_back = jnp.concatenate(
        [jnp.where((depth == d + 1)[:, None], up, 0.0) for d in range(NREC)], axis=1
    ).astype(bf16)
    grads = jnp.concatenate([gate[:, None] * up, gate[:, None] * adapter_scale * down], axis=1).astype(bf16)
    grads_both = jnp.concatenate([grads, flip(grads, 0)], axis=0)

    half = width // 2
    order = [g ^ (g >> 1) for g in range(chips)]

    def columns(values, size, wanted):
        spots = [order.index(m) for m in wanted]
        lo, hi = min(spots), max(spots)
        if hi - lo + 1 == len(spots):
            return values[:, lo * size : (hi + 1) * size], [order[i] for i in range(lo, hi + 1)]
        return jnp.concatenate([values[:, i * size : (i + 1) * size] for i in spots], axis=1), wanted

    def scatter(left, right, size, bits):
        everything = list(range(chips))
        first = bits[0] - 1
        away, away_at = columns(left, size, [m for m in everything if m >> first & 1])
        stay, stay_at = columns(left, size, [m for m in everything if not m >> first & 1])
        sent = flip(dot_rows(away, right).astype(bf16), bits[0])
        kept = dot_rows(stay, right)
        sums = {}
        for i, m in enumerate(stay_at):
            at = away_at.index(m | 1 << first)
            sums[m] = kept[i * size : (i + 1) * size] + sent[at * size : (at + 1) * size].astype(f32)
        for bit in bits[1:]:
            b = 1 << (bit - 1)
            moving = [m for m in sums if m & b]
            sent = flip(jnp.concatenate([sums[m] for m in moving], axis=0).astype(bf16), bit)
            for i, m in enumerate(moving):
                sums[m ^ b] = sums[m ^ b] + sent[i * size : (i + 1) * size].astype(f32)
                del sums[m]
        return sums[0]

    def rank_columns(values):
        parts = []
        for m in order:
            first = ((chip ^ m) * 2 + core) * rank_rows
            part = lax.dynamic_slice_in_dim(values, first % rank, rank_rows, axis=1)
            parts.append(jnp.where((depth_both == (first // rank + 1).astype(f32))[:, None], part, jnp.zeros((), bf16)))
        return jnp.concatenate(parts, axis=1)

    down_grad = scatter(rank_columns(grads_both[:, :rank]), hidden_both, rank_rows, chip_bits)
    up_grad = scatter(rank_columns(grads_both[:, rank:]), dy_both, rank_rows, chip_bits[::-1])

    weight_cut = out_weight.reshape(shards, CHUNKS, cut, width)
    pre = None
    weight_rows = []
    for j in range(CHUNKS):
        whole = gathered[j]

        def of_core(which):
            return jnp.concatenate(
                [
                    lax.dynamic_slice_in_dim(whole, ((chip ^ m) * 2 + which) * cut, cut, axis=1)
                    for m in order
                ],
                axis=1,
            )

        left = jnp.concatenate([of_core(core), flip(of_core(1 - core), 0)], axis=0)
        weight_rows.append(
            jnp.concatenate(
                [
                    scatter(left, gated_hidden[:, :half], cut, chip_bits),
                    scatter(left, gated_hidden[:, half:], cut, chip_bits[::-1]),
                ],
                axis=1,
            )
        )
        term = jnp.dot(whole, weight_cut[:, j].reshape(shards * cut, width), preferred_element_type=f32)
        pre = term if pre is None else pre + term
    weight_grad = jnp.concatenate(weight_rows, axis=0)

    pre = pre + jnp.dot(wide_back, downs_t, preferred_element_type=f32)
    hidden_grad = gate[:, None] * pre
    gate_grad = lax.psum(jnp.sum(hidden.astype(f32) * pre, axis=1), "tp")
    return (hidden_grad, gate_grad, weight_grad, down_grad, up_grad)


def solution(mesh):
    in_specs = (
        P("seq", "tp"),
        P("seq", "tp"),
        P("seq"),
        P("seq"),
        P(),
        P(None, "tp"),
        P("tp", "seq"),
        P("seq", "tp"),
    )
    out_specs = (P("seq", "tp"), P("seq"), P("seq", "tp"), P("seq", "tp"), P("seq", "tp"))
    return jax.shard_map(local, mesh=mesh, in_specs=in_specs, out_specs=out_specs, check_vma=False)
```

time: 943 us -> 573 us (0.61)
  waiting for transfers between devices: 713 us -> 148 us
  other arithmetic: 20 us -> 110 us
  starting transfers between devices: 26.2 us -> 87.3 us
  matrix products: 85.5 us -> 125 us
  local copies, waits for them, and re-layouts: 64.4 us -> 78.3 us
  between operations: 14.6 us -> 2.76 us
    reduce_scatter x3 -> x0, waiting for transfers between devices: 385 us -> none  [the longest x1 385 us: local(): lax.psum_scatter(lax.dot_general(gated_dy, rows_h, contract_rows, preferr...]
    all_to_all x6 -> x0, waiting for transfers between devices: 184 us -> none  [the longest x1 97.2 us: local(): lax.all_to_all(grad_slots.reshape(per_pair, shards, width_local), 'seq',...]
    ppermute x0 -> x64, waiting for transfers between devices: none -> 148 us  [the longest x12 85.5 us: gather_line(): lax.ppermute(downs[-1], 'tp', [(i, i - 1) for i in range(1, size - k + 1)])]
    all_gather x3 -> x0, waiting for transfers between devices: 98.6 us -> none  [the longest x1 98.6 us: local(): full_dy = lax.all_gather(rows_dy, 'tp', axis=1, tiled=True)]
    ppermute x0 -> x64, starting transfers between devices: none -> 87.3 us  [the longest x12 28.4 us: gather_line(): lax.ppermute(ups[-1], 'tp', [(i, i + 1) for i in range(k - 1, size - 1)])]
    concatenate x0 -> x18, other arithmetic: none -> 69.3 us  [the longest x4 36.4 us: local(): left = jnp.concatenate([of_core(core), flip(of_core(1 - core), 0)], axis=0)]
    psum x1 -> x0, waiting for transfers between devices: 42.7 us -> none  [local(): lax.psum((select_block(down_part, selector), select_block(up_part, select...]
    dot_general x7 -> x27, matrix products: 85.5 us -> 125 us  [the longest x4 55.7 us: local(): jnp.dot(whole, weight_cut[:, j].reshape(shards * cut, width), preferred_e...]
  transfers between devices with their start and end apart: 13 -> 64, of which waited for: 7 -> 17; matrix products, arithmetic and copies ran while one was open for 16% -> 53% of each run, Pallas kernels for 0% -> 0%
where the time goes in v1:
time: 573 us; the launch traced here: 564 us
  waiting for transfers between devices  148 us (26%)
  matrix products  125 us (22%)
  other arithmetic  110 us (19%)
  starting transfers between devices  87.3 us (15%)
  local copies, waits for them, and re-layouts  78.3 us (14%)
  blocking collectives  12 us (2%)
    ppermute x12, waiting for transfers between devices, gather_line(): lax.ppermute(downs[-1], 'tp', [(i, i - 1) for i in range(1, size - k + 1)])  85.5 us
    dot_general x4, matrix products, local(): jnp.dot(whole, weight_cut[:, j].reshape(shards * cut, width), preferred_e...  55.7 us
    dot_general x20, matrix products, dot_rows(): return lax.dot_general(a, b, contract_rows, preferred_element_type=f32)  50.3 us
    ppermute x34, waiting for transfers between devices, flip(): return lax.ppermute(value, 'seq', [(i, i ^ 1 << bit) for i in range(size)])  44.7 us
    concatenate x4, other arithmetic, local(): left = jnp.concatenate([of_core(core), flip(of_core(1 - core), 0)], axis=0)  36.4 us
    unnamed x167, local copies, waits for them, and re-layouts  32.9 us
    ppermute x12, starting transfers between devices, gather_line(): lax.ppermute(ups[-1], 'tp', [(i, i + 1) for i in range(k - 1, size - 1)])  28.4 us
    ppermute x34, starting transfers between devices, flip(): return lax.ppermute(value, 'seq', [(i, i ^ 1 << bit) for i in range(size)])  26.4 us
  transfers between devices with their start and end apart: 64, of which 17 were waited for; matrix products, arithmetic and copies ran while one was open for 53% of the time, Pallas kernels for 0%

profile of v1, /device:TPU:0, one launch (start us, length us, event | category | flops | bytes accessed | tf_op | source)
XLA Modules:
  0.0 563.8 jit_solution(12118127634832625006)
XLA Ops:
  10.4 5.8 %collective-permute-start = (bf16[768,512]{0,1:T(8,128)(2,1)}, bf16[768,512]{0,1:T(8,128)(2,1)}, u32[]{:S(2)}, u32[]{:S(2)}) collective-permute-start(bf16[768,512]{0,1:T(8,128)(2,1)} %bitcast.2), channel_id=1, source_target_pairs={{0,1},{1,2},{2,3},{4,5},{5,6},{6,7},{8,9},{9,10},{10,11},{12,13},{... | collective-permute-start | bytes 2359304 | tf_op jit(solution)/shard_map/ppermute | solution.py:54
  22.7 23.2 %fusion.158 = (bf16[8,1,256,2048]{3,2,1,0:T(8,128)(2,1)}, bf16[8,1,256,2048]{3,2,1,0:T(8,128)(2,1)}, bf16[8,1,256,2048]{3,2,1,0:T(8,128)(2,1)}, bf16[8,1,256,2048]{3,2,1,0:T(8,128)(2,1)}) fusion(bf16[8,4,256,2048]{3,2,1,0:T(8,128)(2,1)} %bitcast.30), kind=kLoop, calls=%fused_computation.303 | loop fusion | bytes 67108864 | tf_op jit(solution)/shard_map/slice | solution.py:195
  60.8 6.8 %collective-permute-start.6 = (bf16[768,512]{0,1:T(8,128)(2,1)}, bf16[768,512]{0,1:T(8,128)(2,1)S(1)}, u32[]{:S(2)}, u32[]{:S(2)}) collective-permute-start(bf16[768,512]{0,1:T(8,128)(2,1)} %bitcast.62), channel_id=1, source_target_pairs={{0,1},{1,2},{2,3},{4,5},{5,6},{6,7},{8,9},{9,10},{10,11},{12,13},{... | collective-permute-start | bytes 2359304 | tf_op jit(solution)/shard_map/ppermute | solution.py:54
  68.9 6.5 %collective-permute-done.25 = bf16[2,128,2048]{2,1,0:T(8,128)(2,1)} collective-permute-done((bf16[2,128,2048]{2,1,0:T(8,128)(2,1)}, bf16[2,128,2048]{2,1,0:T(8,128)(2,1)}, u32[]{:S(2)}, u32[]{:S(2)}) %collective-permute-start.25) | collective-permute-done | bytes 1048608 | tf_op jit(solution)/shard_map/ppermute | solution.py:21
  84.5 5.7 %collective-permute-done.9 = bf16[768,512]{0,1:T(8,128)(2,1)S(1)} collective-permute-done((bf16[768,512]{0,1:T(8,128)(2,1)}, bf16[768,512]{0,1:T(8,128)(2,1)S(1)}, u32[]{:S(2)}, u32[]{:S(2)}) %collective-permute-start.9) | collective-permute-done | bytes 786464 | tf_op jit(solution)/shard_map/ppermute | solution.py:55
  95.8 11.3 %collective-permute-done.4 = bf16[768,512]{0,1:T(8,128)(2,1)S(1)} collective-permute-done((bf16[768,512]{0,1:T(8,128)(2,1)}, bf16[768,512]{0,1:T(8,128)(2,1)S(1)}, u32[]{:S(2)}, u32[]{:S(2)}) %collective-permute-start.4) | collective-permute-done | bytes 786464 | tf_op jit(solution)/shard_map/ppermute | solution.py:55
  114.3 24.8 %collective-permute-done.5 = bf16[768,512]{0,1:T(8,128)(2,1)S(1)} collective-permute-done((bf16[768,512]{0,1:T(8,128)(2,1)S(1)}, bf16[768,512]{0,1:T(8,128)(2,1)S(1)}, u32[]{:S(2)}, u32[]{:S(2)}) %collective-permute-start.5) | collective-permute-done | bytes 786464 | tf_op jit(solution)/shard_map/ppermute | solution.py:55
  141.2 9.0 %fusion.8 = f32[768,2048]{1,0:T(8,128)} fusion(bf16[2048,2048]{1,0:T(8,128)(2,1)S(1)} %bitcast.49, bf16[768,3584]{0,1:T(8,128)(2,1)S(1)} %constant_dynamic-update-slice_fusion, s32[]{:T(128)S(6)} %select_n.211), kind=kOutput, calls=%fused_computation.23 | convolution fusion | flops 6442450944 | bytes 17825796 | tf_op jit(solution)/shard_map/dot_general | solution.py:195
  153.8 5.1 collective-permute-done.10
  164.9 17.2 %collective-permute-done.11 = bf16[768,512]{0,1:T(8,128)(2,1)S(1)} collective-permute-done((bf16[768,512]{0,1:T(8,128)(2,1)S(1)}, bf16[768,512]{0,1:T(8,128)(2,1)S(1)}, u32[]{:S(2)}, u32[]{:S(2)}) %collective-permute-start.11) | collective-permute-done | bytes 786464 | tf_op jit(solution)/shard_map/ppermute | solution.py:55
  183.7 9.1 %fusion.6 = f32[768,2048]{1,0:T(8,128)} fusion(bf16[2048,2048]{1,0:T(8,128)(2,1)S(1)} %bitcast.46, bf16[768,3584]{0,1:T(8,128)(2,1)S(1)} %constant_dynamic-update-slice_fusion.7, s32[]{:T(128)S(6)} %select_n.211), kind=kOutput, calls=%fused_computation.21 | convolution fusion | flops 6442450944 | bytes 17825796 | tf_op jit(solution)/shard_map/dot_general | solution.py:195
  204.1 5.1 gather_fusion
  209.2 8.3 %convolution_bitcast_fusion = f32[768,1024]{0,1:T(8,128)} fusion(bf16[1024,2048]{1,0:T(8,128)(2,1)} %bitcast.56, bf16[768,2048]{1,0:T(8,128)(2,1)} %param.12), kind=kOutput, calls=%fused_computation.35 | convolution fusion | flops 3221225472 | bytes 10485760 | tf_op jit(solution)/shard_map/dot_general | solution.py:119
  226.8 5.1 gather_fusion.1
  231.9 5.4 fusion.165
  238.7 11.9 %collective-permute-start.30 = (bf16[768,512]{0,1:T(8,128)(2,1)}, bf16[768,512]{0,1:T(8,128)(2,1)S(1)}, u32[]{:S(2)}, u32[]{:S(2)}) collective-permute-start(bf16[768,512]{0,1:T(8,128)(2,1)} %fusion.143), channel_id=1, source_target_pairs={{0,1},{4,5},{8,9},{12,13},{16,17},{20,21},{24,25},{28,29}} | collective-permute-start | bytes 2359304 | tf_op jit(solution)/shard_map/ppermute | solution.py:65
  256.8 7.4 %collective-permute-done.17 = bf16[768,512]{0,1:T(8,128)(2,1)} collective-permute-done((bf16[768,512]{0,1:T(8,128)(2,1)}, bf16[768,512]{0,1:T(8,128)(2,1)}, u32[]{:S(2)}, u32[]{:S(2)}) %collective-permute-start.17) | collective-permute-done | bytes 786464 | tf_op jit(solution)/shard_map/ppermute | solution.py:55
  271.3 17.8 %fusion.4 = f32[768,2048]{1,0:T(8,128)} fusion(bf16[2048,2048]{1,0:T(8,128)(2,1)S(1)} %bitcast.43, bf16[768,3584]{0,1:T(8,128)(2,1)S(1)} %constant_dynamic-update-slice_fusion.14, s32[]{:T(128)S(6)} %select_n.211), kind=kOutput, calls=%fused_computation.19 | convolution fusion | flops 6442450944 | bytes 17825796 | tf_op jit(solution)/shard_map/dot_general | solution.py:195
  289.1 7.6 %pad_maximum_fusion.5 = bf16[1536,1024]{0,1:T(8,128)(2,1)S(1)} fusion(bf16[768,1024]{0,1:T(8,128)(2,1)} %collective-permute-done.36, bf16[768,256]{0,1:T(8,128)(2,1)S(1)} %copy-done.32, bf16[768,256]{0,1:T(8,128)(2,1)S(1)} %copy-done.33, bf16[768,256]{0,1:T(8,128)(2,1)} %get-tuple-element.29, bf16[768,256]{0,1:T(8,128)(2,1)S(1)} %copy-done.31), kind=kLoop, calls=%fused_computation.13 | loop fusion | flops 15728640 | bytes 6291456 | tf_op jit(solution)/shard_map/concatenate | solution.py:185
  317.0 14.0 %collective-permute-done.23 = bf16[768,512]{0,1:T(8,128)(2,1)S(1)} collective-permute-done((bf16[768,512]{0,1:T(8,128)(2,1)}, bf16[768,512]{0,1:T(8,128)(2,1)S(1)}, u32[]{:S(2)}, u32[]{:S(2)}) %collective-permute-start.23) | collective-permute-done | bytes 786464 | tf_op jit(solution)/shard_map/ppermute | solution.py:55
  339.1 9.0 %pad_maximum_fusion.7 = bf16[1536,1024]{0,1:T(8,128)(2,1)S(1)} fusion(bf16[768,1024]{0,1:T(8,128)(2,1)S(1)} %collective-permute-done.48, bf16[768,256]{0,1:T(8,128)(2,1)S(1)} %get-tuple-element.43, bf16[768,256]{0,1:T(8,128)(2,1)S(1)} %get-tuple-element.44, bf16[768,256]{0,1:T(8,128)(2,1)S(1)} %get-tuple-element.45, bf16[768,256]{0,1:T(8,128)(2,1)S(1)} %get-tuple-element.38), kind=kLoop, calls=%fused_computation.15 | loop fusion | flops 15728640 | bytes 6291456 | tf_op jit(solution)/shard_map/concatenate | solution.py:185
  355.7 9.8 %pad_maximum_fusion.6 = bf16[1536,1024]{0,1:T(8,128)(2,1)S(1)} fusion(bf16[768,1024]{0,1:T(8,128)(2,1)S(1)} %collective-permute-done.43, bf16[768,256]{0,1:T(8,128)(2,1)S(1)} %get-tuple-element.96, bf16[768,256]{0,1:T(8,128)(2,1)S(1)} %get-tuple-element.95, bf16[768,256]{0,1:T(8,128)(2,1)S(1)} %get-tuple-element.94, bf16[768,256]{0,1:T(8,128)(2,1)S(1)} %get-tuple-element.101), kind=kLoop, calls=%fused_computation.14 | loop fusion | flops 15728640 | bytes 6291456 | tf_op jit(solution)/shard_map/concatenate | solution.py:185
  383.9 10.0 %pad_maximum_fusion.8 = bf16[1536,1024]{0,1:T(8,128)(2,1)S(1)} fusion(bf16[768,1024]{0,1:T(8,128)(2,1)S(1)} %collective-permute-done.53, bf16[768,256]{0,1:T(8,128)(2,1)S(1)} %get-tuple-element.51, bf16[768,256]{0,1:T(8,128)(2,1)S(1)} %get-tuple-element.52, bf16[768,256]{0,1:T(8,128)(2,1)S(1)} %get-tuple-element.53, bf16[768,256]{0,1:T(8,128)(2,1)S(1)} %get-tuple-element.46), kind=kLoop, calls=%fused_computation.16 | loop fusion | flops 15728640 | bytes 6291456 | tf_op jit(solution)/shard_map/concatenate | solution.py:185
  409.8 9.2 %collective-permute-done.46 = bf16[512,1024]{1,0:T(8,128)(2,1)S(1)} collective-permute-done((bf16[512,1024]{1,0:T(8,128)(2,1)S(1)}, bf16[512,1024]{1,0:T(8,128)(2,1)S(1)}, u32[]{:S(2)}, u32[]{:S(2)}) %collective-permute-start.46) | collective-permute-done | bytes 1048608 | tf_op jit(solution)/shard_map/ppermute | solution.py:21
  427.0 17.3 %collective-permute-done.35 = bf16[768,512]{0,1:T(8,128)(2,1)S(1)} collective-permute-done((bf16[768,512]{0,1:T(8,128)(2,1)S(1)}, bf16[768,512]{0,1:T(8,128)(2,1)S(1)}, u32[]{:S(2)}, u32[]{:S(2)}) %collective-permute-start.35) | collective-permute-done | bytes 786464 | tf_op jit(solution)/shard_map/ppermute | solution.py:66
  447.4 5.4 fusion.39
  452.9 19.8 %multiply_reduce_fusion = (f32[768]{0:T(1024)S(1)}, f32[768,2048]{1,0:T(8,128)}) fusion(bf16[768,2048]{1,0:T(8,128)(2,1)S(1)} %copy-done.15, f32[768]{0:T(1024)S(1)} %copy-done.54, f32[768,2048]{1,0:T(8,128)} %fusion.39, bf16[2048,2048]{1,0:T(8,128)(2,1)} %bitcast.40, bf16[768,3584]{0,1:T(8,128)(2,1)} %copy-done.17, s32[]{:T(128)S(6)} %select_n.211, ...), kind=kOutput, calls=%fused_computation.7 | convolution fusion | flops 6455032832 | bytes 46143492 | tf_op jit(solution)/shard_map/dot_general | solution.py:195
  472.7 12.0 %psum.7 = f32[768]{0:T(1024)} all-reduce(f32[768]{0:T(1024)S(1)} %get-tuple-element.20), channel_id=1, replica_groups=mesh['seq'=8,'tp'=4] {'tp'}, use_global_device_ids=true, to_apply=%region_1.3 | all-reduce | flops 768 | bytes 6144 | tf_op jit(solution)/shard_map/psum | solution.py:201
  514.2 5.8 %fusion.1 = f32[256,2048]{1,0:T(8,128)} fusion(bf16[768,2048]{0,1:T(8,128)(2,1)} %collective-permute-done.61, bf16[768,2048]{0,1:T(8,128)(2,1)S(1)} %broadcast_select_fusion, bf16[1536,128]{0,1:T(8,128)(2,1)S(1)} %get-tuple-element.85, bf16[1536,128]{0,1:T(8,128)(2,1)S(1)} %get-tuple-element.84), kind=kOutput, calls=%fused_computation.12 | convolution fusion | flops 1624768512 | bytes 9175040 | tf_op jit(solution)/shard_map/dot_general | solution.py:16
  522.8 11.4 %collective-permute-done.59 = bf16[256,2048]{1,0:T(8,128)(2,1)S(1)} collective-permute-done((bf16[256,2048]{1,0:T(8,128)(2,1)S(1)}, bf16[256,2048]{1,0:T(8,128)(2,1)S(1)}, u32[]{:S(2)}, u32[]{:S(2)}) %collective-permute-start.59) | collective-permute-done | bytes 1048608 | tf_op jit(solution)/shard_map/ppermute | solution.py:21
  536.2 12.2 %maximum_maximum_fusion = f32[1024,2048]{1,0:T(8,128)} fusion(f32[256,1024]{1,0:T(8,128)S(1)} %fusion.92, f32[256,1024]{1,0:T(8,128)S(1)} %fusion.94, f32[256,1024]{1,0:T(8,128)S(1)} %fusion.96, f32[256,1024]{1,0:T(8,128)S(1)} %fusion.98, f32[256,1024]{1,0:T(8,128)S(1)} %fusion.100, f32[256,1024]{1,0:T(8,128)S(1)} %fusion.102, f32[256,1024]{1,0:T(8,128)S(1)} %copy-done.6, ...), kind=kLoop, calls=%fused_computation.5 | loop fusion | flops 14680064 | bytes 16777216 | tf_op jit(solution)/shard_map/concatenate | solution.py:197
  553.5 7.6 %collective-permute-done.63 = bf16[128,2048]{1,0:T(8,128)(2,1)S(1)} collective-permute-done((bf16[128,2048]{1,0:T(8,128)(2,1)S(1)}, bf16[128,2048]{1,0:T(8,128)(2,1)S(1)}, u32[]{:S(2)}, u32[]{:S(2)}) %collective-permute-start.63) | collective-permute-done | bytes 524320 | tf_op jit(solution)/shard_map/ppermute | solution.py:21
  (382 shorter events, 224.6 us)
Async XLA Ops:
  10.4 40.3 %collective-permute-start = (bf16[768,512]{0,1:T(8,128)(2,1)}, bf16[768,512]{0,1:T(8,128)(2,1)}, u32[]{:S(2)}, u32[]{:S(2)}) collective-permute-start(bf16[768,512]{0,1:T(8,128)(2,1)} %bitcast.2), channel_id=1, source_target_pairs={{0,1},{1,2},{2,3},{4,5},{5,6},{6,7},{8,9},{9,10},{10,11},{12,13},{... | collective-permute-start | bytes 2359304 | tf_op jit(solution)/shard_map/ppermute | solution.py:54
  16.2 44.6 %collective-permute-start.3 = (bf16[768,512]{0,1:T(8,128)(2,1)}, bf16[768,512]{0,1:T(8,128)(2,1)}, u32[]{:S(2)}, u32[]{:S(2)}) collective-permute-start(bf16[768,512]{0,1:T(8,128)(2,1)} %bitcast.2), channel_id=1, source_target_pairs={{1,0},{2,1},{3,2},{5,4},{6,5},{7,6},{9,8},{10,9},{11,10},{13,12},{... | collective-permute-start | bytes 2359304 | tf_op jit(solution)/shard_map/ppermute | solution.py:55
  21.0 31.8 %collective-permute-start.27 = (bf16[1,128,2048]{2,1,0:T(8,128)(2,1)}, bf16[1,128,2048]{2,1,0:T(8,128)(2,1)}, u32[]{:S(2)}, u32[]{:S(2)}) collective-permute-start(bf16[1,128,2048]{2,1,0:T(8,128)(2,1)} %bitcast.52), channel_id=1, source_target_pairs={{0,16},{4,20},{8,24},{12,28},{16,0},{20,4},{24,8},{28,12},{1,17},{... | collective-permute-start | bytes 1572872 | tf_op jit(solution)/shard_map/ppermute | solution.py:21
  22.6 45.0 %collective-permute-start.37 = (bf16[2,768]{1,0:T(2,128)(2,1)S(1)}, bf16[2,768]{1,0:T(2,128)(2,1)S(1)}, u32[]{:S(2)}, u32[]{:S(2)}) collective-permute-start(bf16[2,768]{1,0:T(2,128)(2,1)S(1)} %pad_maximum_fusion.23), channel_id=1, source_target_pairs={{0,4},{4,0},{8,12},{12,8},{16,20},{20,16},{24,28},{28,24},{1,5},{5... | collective-permute-start | bytes 9224 | tf_op jit(solution)/shard_map/ppermute | solution.py:21
  80.7 112.2 %collective-permute-start.38 = (bf16[768,2048]{1,0:T(8,128)(2,1)S(1)}, bf16[768,2048]{1,0:T(8,128)(2,1)S(1)}, u32[]{:S(2)}, u32[]{:S(2)}) collective-permute-start(bf16[768,2048]{1,0:T(8,128)(2,1)S(1)} %copy-done.14), channel_id=1, source_target_pairs={{0,4},{4,0},{8,12},{12,8},{16,20},{20,16},{24,28},{28,24},{1,5},{5... | collective-permute-start | bytes 9437192 | tf_op jit(solution)/shard_map/ppermute | solution.py:21
  90.2 60.0 %collective-permute-start.12 = (bf16[768,512]{0,1:T(8,128)(2,1)S(1)}, bf16[768,512]{0,1:T(8,128)(2,1)}, u32[]{:S(2)}, u32[]{:S(2)}) collective-permute-start(bf16[768,512]{0,1:T(8,128)(2,1)S(1)} %bitcast.59), channel_id=1, source_target_pairs={{0,1},{1,2},{2,3},{4,5},{5,6},{6,7},{8,9},{9,10},{10,11},{12,13},{... | collective-permute-start | bytes 2359304 | tf_op jit(solution)/shard_map/ppermute | solution.py:54
  94.5 55.7 %collective-permute-start.15 = (bf16[768,512]{0,1:T(8,128)(2,1)S(1)}, bf16[768,512]{0,1:T(8,128)(2,1)}, u32[]{:S(2)}, u32[]{:S(2)}) collective-permute-start(bf16[768,512]{0,1:T(8,128)(2,1)S(1)} %bitcast.60), channel_id=1, source_target_pairs={{1,0},{2,1},{3,2},{5,4},{6,5},{7,6},{9,8},{10,9},{11,10},{13,12},{... | collective-permute-start | bytes 2359304 | tf_op jit(solution)/shard_map/ppermute | solution.py:55
  107.1 33.3 %collective-permute-start.7 = (bf16[768,512]{0,1:T(8,128)(2,1)S(1)}, bf16[768,512]{0,1:T(8,128)(2,1)S(1)}, u32[]{:S(2)}, u32[]{:S(2)}) collective-permute-start(bf16[768,512]{0,1:T(8,128)(2,1)S(1)} %collective-permute-done.6), channel_id=1, source_target_pairs={{1,2},{2,3},{5,6},{6,7},{9,10},{10,11},{13,14},{14,15},{17,18},{18... | collective-permute-start | bytes 2359304 | tf_op jit(solution)/shard_map/ppermute | solution.py:54
  150.2 49.0 %collective-permute-start.26 = (bf16[4,128,2048]{2,1,0:T(8,128)(2,1)S(1)}, bf16[4,128,2048]{2,1,0:T(8,128)(2,1)}, u32[]{:S(2)}, u32[]{:S(2)}) collective-permute-start(bf16[4,128,2048]{2,1,0:T(8,128)(2,1)S(1)} %pad_maximum_fusion.11), channel_id=1, source_target_pairs={{0,4},{4,0},{8,12},{12,8},{16,20},{20,16},{24,28},{28,24},{1,5},{5... | collective-permute-start | bytes 6291464 | tf_op jit(solution)/shard_map/ppermute | solution.py:21
  150.2 71.7 %collective-permute-start.29 = (bf16[4,128,2048]{2,1,0:T(8,128)(2,1)}, bf16[4,128,2048]{2,1,0:T(8,128)(2,1)}, u32[]{:S(2)}, u32[]{:S(2)}) collective-permute-start(bf16[4,128,2048]{2,1,0:T(8,128)(2,1)} %pad_maximum_fusion.12), channel_id=1, source_target_pairs={{0,4},{4,0},{8,12},{12,8},{16,20},{20,16},{24,28},{28,24},{1,5},{5... | collective-permute-start | bytes 6291464 | tf_op jit(solution)/shard_map/ppermute | solution.py:21
  158.9 58.6 %collective-permute-start.18 = (bf16[768,512]{0,1:T(8,128)(2,1)}, bf16[768,512]{0,1:T(8,128)(2,1)}, u32[]{:S(2)}, u32[]{:S(2)}) collective-permute-start(bf16[768,512]{0,1:T(8,128)(2,1)} %bitcast.9), channel_id=1, source_target_pairs={{0,1},{1,2},{2,3},{4,5},{5,6},{6,7},{8,9},{9,10},{10,11},{12,13},{... | collective-permute-start | bytes 2359304 | tf_op jit(solution)/shard_map/ppermute | solution.py:54
  182.1 35.4 %collective-permute-start.21 = (bf16[768,512]{0,1:T(8,128)(2,1)}, bf16[768,512]{0,1:T(8,128)(2,1)}, u32[]{:S(2)}, u32[]{:S(2)}) collective-permute-start(bf16[768,512]{0,1:T(8,128)(2,1)} %bitcast.9), channel_id=1, source_target_pairs={{1,0},{2,1},{3,2},{5,4},{6,5},{7,6},{9,8},{10,9},{11,10},{13,12},{... | collective-permute-start | bytes 2359304 | tf_op jit(solution)/shard_map/ppermute | solution.py:55
  217.4 71.7 %collective-permute-start.36 = (bf16[768,1024]{0,1:T(8,128)(2,1)}, bf16[768,1024]{0,1:T(8,128)(2,1)}, u32[]{:S(2)}, u32[]{:S(2)}) collective-permute-start(bf16[768,1024]{0,1:T(8,128)(2,1)} %pad_maximum_fusion.14), channel_id=1, source_target_pairs={{0,4},{4,0},{8,12},{12,8},{16,20},{20,16},{24,28},{28,24},{1,5},{5... | collective-permute-start | bytes 4718600 | tf_op jit(solution)/shard_map/ppermute | solution.py:21
  217.4 85.8 %collective-permute-start.19 = (bf16[768,512]{0,1:T(8,128)(2,1)}, bf16[768,512]{0,1:T(8,128)(2,1)}, u32[]{:S(2)}, u32[]{:S(2)}) collective-permute-start(bf16[768,512]{0,1:T(8,128)(2,1)} %collective-permute-done.18), channel_id=1, source_target_pairs={{1,2},{2,3},{5,6},{6,7},{9,10},{10,11},{13,14},{14,15},{17,18},{18... | collective-permute-start | bytes 2359304 | tf_op jit(solution)/shard_map/ppermute | solution.py:54
  219.0 89.5 %collective-permute-start.22 = (bf16[768,512]{0,1:T(8,128)(2,1)}, bf16[768,512]{0,1:T(8,128)(2,1)}, u32[]{:S(2)}, u32[]{:S(2)}) collective-permute-start(bf16[768,512]{0,1:T(8,128)(2,1)} %collective-permute-done.21), channel_id=1, source_target_pairs={{1,0},{2,1},{5,4},{6,5},{9,8},{10,9},{13,12},{14,13},{17,16},{18,1... | collective-permute-start | bytes 2359304 | tf_op jit(solution)/shard_map/ppermute | solution.py:55
  221.9 42.3 %collective-permute-start.17 = (bf16[768,512]{0,1:T(8,128)(2,1)}, bf16[768,512]{0,1:T(8,128)(2,1)}, u32[]{:S(2)}, u32[]{:S(2)}) collective-permute-start(bf16[768,512]{0,1:T(8,128)(2,1)} %collective-permute-done.16), channel_id=1, source_target_pairs={{1,0},{5,4},{9,8},{13,12},{17,16},{21,20},{25,24},{29,28}} | collective-permute-start | bytes 2359304 | tf_op jit(solution)/shard_map/ppermute | solution.py:55
  238.7 68.1 %collective-permute-start.30 = (bf16[768,512]{0,1:T(8,128)(2,1)}, bf16[768,512]{0,1:T(8,128)(2,1)S(1)}, u32[]{:S(2)}, u32[]{:S(2)}) collective-permute-start(bf16[768,512]{0,1:T(8,128)(2,1)} %fusion.143), channel_id=1, source_target_pairs={{0,1},{4,5},{8,9},{12,13},{16,17},{20,21},{24,25},{28,29}} | collective-permute-start | bytes 2359304 | tf_op jit(solution)/shard_map/ppermute | solution.py:65
  264.2 71.8 %collective-permute-start.33 = (bf16[768,512]{0,1:T(8,128)(2,1)}, bf16[768,512]{0,1:T(8,128)(2,1)S(1)}, u32[]{:S(2)}, u32[]{:S(2)}) collective-permute-start(bf16[768,512]{0,1:T(8,128)(2,1)} %fusion.143), channel_id=1, source_target_pairs={{3,2},{7,6},{11,10},{15,14},{19,18},{23,22},{27,26},{31,30}} | collective-permute-start | bytes 2359304 | tf_op jit(solution)/shard_map/ppermute | solution.py:66
  289.1 49.5 %collective-permute-start.48 = (bf16[768,1024]{0,1:T(8,128)(2,1)S(1)}, bf16[768,1024]{0,1:T(8,128)(2,1)S(1)}, u32[]{:S(2)}, u32[]{:S(2)}) collective-permute-start(bf16[768,1024]{0,1:T(8,128)(2,1)S(1)} %pad_maximum_fusion.16), channel_id=1, source_target_pairs={{0,4},{4,0},{8,12},{12,8},{16,20},{20,16},{24,28},{28,24},{1,5},{5... | collective-permute-start | bytes 4718600 | tf_op jit(solution)/shard_map/ppermute | solution.py:21
  334.3 172.6 %collective-permute-start.61 = (bf16[768,2048]{0,1:T(8,128)(2,1)S(1)}, bf16[768,2048]{0,1:T(8,128)(2,1)}, u32[]{:S(2)}, u32[]{:S(2)}) collective-permute-start(bf16[768,2048]{0,1:T(8,128)(2,1)S(1)} %broadcast_select_fusion), channel_id=1, source_target_pairs={{0,4},{4,0},{8,12},{12,8},{16,20},{20,16},{24,28},{28,24},{1,5},{5... | collective-permute-start | bytes 9437192 | tf_op jit(solution)/shard_map/ppermute | solution.py:21
  336.0 46.7 %collective-permute-start.53 = (bf16[768,1024]{0,1:T(8,128)(2,1)S(1)}, bf16[768,1024]{0,1:T(8,128)(2,1)S(1)}, u32[]{:S(2)}, u32[]{:S(2)}) collective-permute-start(bf16[768,1024]{0,1:T(8,128)(2,1)S(1)} %pad_maximum_fusion.17), channel_id=1, source_target_pairs={{0,4},{4,0},{8,12},{12,8},{16,20},{20,16},{24,28},{28,24},{1,5},{5... | collective-permute-start | bytes 4718600 | tf_op jit(solution)/shard_map/ppermute | solution.py:21
  336.1 35.0 %collective-permute-start.42 = (bf16[256,1024]{1,0:T(8,128)(2,1)}, bf16[256,1024]{1,0:T(8,128)(2,1)}, u32[]{:S(2)}, u32[]{:S(2)}) collective-permute-start(bf16[256,1024]{1,0:T(8,128)(2,1)} %fusion.103), channel_id=1, source_target_pairs={{0,8},{4,12},{8,0},{12,4},{16,24},{20,28},{24,16},{28,20},{1,9},{5... | collective-permute-start | bytes 1572872 | tf_op jit(solution)/shard_map/ppermute | solution.py:21
  338.6 38.2 %collective-permute-start.40 = (bf16[256,1024]{1,0:T(8,128)(2,1)S(1)}, bf16[256,1024]{1,0:T(8,128)(2,1)}, u32[]{:S(2)}, u32[]{:S(2)}) collective-permute-start(bf16[256,1024]{1,0:T(8,128)(2,1)S(1)} %fusion.105), channel_id=1, source_target_pairs={{0,16},{4,20},{8,24},{12,28},{16,0},{20,4},{24,8},{28,12},{1,17},{... | collective-permute-start | bytes 1572872 | tf_op jit(solution)/shard_map/ppermute | solution.py:21
  371.1 34.7 %collective-permute-start.51 = (bf16[512,1024]{1,0:T(8,128)(2,1)}, bf16[512,1024]{1,0:T(8,128)(2,1)S(1)}, u32[]{:S(2)}, u32[]{:S(2)}) collective-permute-start(bf16[512,1024]{1,0:T(8,128)(2,1)} %fusion.78), channel_id=1, source_target_pairs={{0,16},{4,20},{8,24},{12,28},{16,0},{20,4},{24,8},{28,12},{1,17},{... | collective-permute-start | bytes 3145736 | tf_op jit(solution)/shard_map/ppermute | solution.py:21
  381.8 37.3 %collective-permute-start.46 = (bf16[512,1024]{1,0:T(8,128)(2,1)S(1)}, bf16[512,1024]{1,0:T(8,128)(2,1)S(1)}, u32[]{:S(2)}, u32[]{:S(2)}) collective-permute-start(bf16[512,1024]{1,0:T(8,128)(2,1)S(1)} %fusion.72), channel_id=1, source_target_pairs={{0,16},{4,20},{8,24},{12,28},{16,0},{20,4},{24,8},{28,12},{1,17},{... | collective-permute-start | bytes 3145736 | tf_op jit(solution)/shard_map/ppermute | solution.py:21
  382.7 41.3 %collective-permute-start.44 = (bf16[512,1024]{1,0:T(8,128)(2,1)S(1)}, bf16[512,1024]{1,0:T(8,128)(2,1)S(1)}, u32[]{:S(2)}, u32[]{:S(2)}) collective-permute-start(bf16[512,1024]{1,0:T(8,128)(2,1)S(1)} %fusion.69), channel_id=1, source_target_pairs={{0,8},{4,12},{8,0},{12,4},{16,24},{20,28},{24,16},{28,20},{1,9},{5... | collective-permute-start | bytes 3145736 | tf_op jit(solution)/shard_map/ppermute | solution.py:21
  407.4 36.8 %collective-permute-start.35 = (bf16[768,512]{0,1:T(8,128)(2,1)S(1)}, bf16[768,512]{0,1:T(8,128)(2,1)S(1)}, u32[]{:S(2)}, u32[]{:S(2)}) collective-permute-start(bf16[768,512]{0,1:T(8,128)(2,1)S(1)} %add_convert_fusion), channel_id=1, source_target_pairs={{1,0},{5,4},{9,8},{13,12},{17,16},{21,20},{25,24},{29,28}} | collective-permute-start | bytes 2359304 | tf_op jit(solution)/shard_map/ppermute | solution.py:66
  419.0 79.0 %collective-permute-start.56 = (bf16[512,1024]{1,0:T(8,128)(2,1)}, bf16[512,1024]{1,0:T(8,128)(2,1)}, u32[]{:S(2)}, u32[]{:S(2)}) collective-permute-start(bf16[512,1024]{1,0:T(8,128)(2,1)} %fusion.84), channel_id=1, source_target_pairs={{0,16},{4,20},{8,24},{12,28},{16,0},{20,4},{24,8},{28,12},{1,17},{... | collective-permute-start | bytes 3145736 | tf_op jit(solution)/shard_map/ppermute | solution.py:21
  423.9 76.7 %collective-permute-start.54 = (bf16[512,1024]{1,0:T(8,128)(2,1)}, bf16[512,1024]{1,0:T(8,128)(2,1)}, u32[]{:S(2)}, u32[]{:S(2)}) collective-permute-start(bf16[512,1024]{1,0:T(8,128)(2,1)} %fusion.81), channel_id=1, source_target_pairs={{0,8},{4,12},{8,0},{12,4},{16,24},{20,28},{24,16},{28,20},{1,9},{5... | collective-permute-start | bytes 3145736 | tf_op jit(solution)/shard_map/ppermute | solution.py:21
  425.8 60.1 %collective-permute-start.52 = (bf16[256,1024]{1,0:T(8,128)(2,1)}, bf16[256,1024]{1,0:T(8,128)(2,1)}, u32[]{:S(2)}, u32[]{:S(2)}) collective-permute-start(bf16[256,1024]{1,0:T(8,128)(2,1)} %fusion.95), channel_id=1, source_target_pairs={{0,8},{4,12},{8,0},{12,4},{16,24},{20,28},{24,16},{28,20},{1,9},{5... | collective-permute-start | bytes 1572872 | tf_op jit(solution)/shard_map/ppermute | solution.py:21
  444.2 44.3 %collective-permute-start.50 = (bf16[256,1024]{1,0:T(8,128)(2,1)}, bf16[256,1024]{1,0:T(8,128)(2,1)}, u32[]{:S(2)}, u32[]{:S(2)}) collective-permute-start(bf16[256,1024]{1,0:T(8,128)(2,1)} %fusion.97), channel_id=1, source_target_pairs={{0,16},{4,20},{8,24},{12,28},{16,0},{20,4},{24,8},{28,12},{1,17},{... | collective-permute-start | bytes 1572872 | tf_op jit(solution)/shard_map/ppermute | solution.py:21
  511.6 36.8 %collective-permute-start.62 = (bf16[256,2048]{1,0:T(8,128)(2,1)}, bf16[256,2048]{1,0:T(8,128)(2,1)}, u32[]{:S(2)}, u32[]{:S(2)}) collective-permute-start(bf16[256,2048]{1,0:T(8,128)(2,1)} %fusion.10), channel_id=1, source_target_pairs={{0,16},{4,20},{8,24},{12,28},{16,0},{20,4},{24,8},{28,12},{1,17},{... | collective-permute-start | bytes 3145736 | tf_op jit(solution)/shard_map/ppermute | solution.py:21
  (102 other events, 1697.6 us)

commit v2 on v1

v2 whole, which is shorter than its diff:
```python
import jax
import jax.numpy as jnp
from jax import lax
from jax.experimental import pallas as pl
from jax.experimental.pallas import tpu as pltpu
from jax.sharding import PartitionSpec as P

NREC = 4
LANES = 128
adapter_scale = 0.5
contract_rows = (((0,), (0,)), ((), ()))
contract_last = (((1,), (1,)), ((), ()))
f32 = jnp.float32
bf16 = jnp.bfloat16


def dot_rows(pairs):
    return sum(
        lax.dot_general(a, b, contract_rows, preferred_element_type=f32) for a, b in pairs
    )


def flip(value, bit):
    size = lax.axis_size("seq")
    return lax.ppermute(value, "seq", [(i, i ^ (1 << bit)) for i in range(size)])


def run(streams):
    results = [None] * len(streams)
    alive = dict(enumerate(streams))
    while alive:
        made = {}
        for i in list(alive):
            try:
                made[i] = alive[i].send(results[i])
            except StopIteration:
                del alive[i]
                results[i] = None
        held = lax.optimization_barrier(made)
        for i, values in held.items():
            results[i] = values


def chunk_sizes(units):
    quarter = max(1, units // 4)
    return [quarter] * (units // quarter)


def add_products(total, terms, closing=None):
    rows, width = terms[0][0].shape[0], terms[0][1].shape[2]
    wide = min(width, 512)
    tiles = width // wide

    def kernel(*refs):
        refs = list(refs)
        done = refs.pop(0)[...] if total is not None else None
        for left, right, _, cut in terms:
            left_ref, right_ref = refs.pop(0), refs.pop(0)
            term = jnp.dot(
                left_ref[...],
                right_ref[...].reshape(right.shape[0] * cut, wide),
                preferred_element_type=f32,
            )
            done = term if done is None else done + term
        if closing is not None:
            scale_ref, hidden_ref, out_ref, sum_ref = refs
            part = jnp.sum(hidden_ref[...].astype(f32) * done, axis=1, keepdims=True)
            first = pl.program_id(0) == 0

            @pl.when(first)
            def _():
                sum_ref[...] = part

            @pl.when(jnp.logical_not(first))
            def _():
                sum_ref[...] += part

            done = scale_ref[...] * done
        else:
            (out_ref,) = refs
        out_ref[...] = done

    in_specs, operands = [], []
    tile = pl.BlockSpec((rows, wide), lambda n: (0, n))
    column = pl.BlockSpec((rows, 1), lambda n: (0, 0))
    if total is not None:
        operands.append(total)
        in_specs.append(tile)
    for left, right, start, cut in terms:
        groups = right.shape[0]
        operands += [left, right]
        in_specs += [
            pl.BlockSpec((rows, groups * cut), lambda n: (0, 0)),
            pl.BlockSpec(
                (pl.Element(groups), pl.Element(cut), pl.Element(wide)),
                lambda n, start=start: (0, start, n * wide),
            ),
        ]
    out_shape, out_specs = [jax.ShapeDtypeStruct((rows, width), f32)], [tile]
    if closing is not None:
        operands += [closing[0][:, None], closing[1]]
        in_specs += [column, tile]
        out_shape.append(jax.ShapeDtypeStruct((rows, 1), f32))
        out_specs.append(column)
    return pl.pallas_call(
        kernel,
        grid=(tiles,),
        in_specs=in_specs,
        out_specs=out_specs,
        out_shape=out_shape,
        input_output_aliases={0: 0} if total is not None else {},
        compiler_params=pltpu.CompilerParams(vmem_limit_bytes=48 * 2**20),
        cost_estimate=pl.CostEstimate(flops=0, bytes_accessed=0, transcendentals=0),
    )(*operands)


def masks_of(bits):
    masks = [0]
    for bit in bits:
        masks = masks + [m | (1 << bit) for m in masks]
    return masks


def column_products(lefts, rights, cut, picks, moving, added=None):
    depth, columns = lefts[0].shape
    half = rights[0].shape[1] // 2
    pairs = len(lefts)
    wide = min(half, 512)
    per = half // wide
    count = len(picks[0])
    kinds = [(moving, bf16)] * (moving > 0) + [(count - moving, f32)] * (count > moving)

    def kernel(*refs):
        left_refs, right_refs, refs = refs[:pairs], refs[pairs : 2 * pairs], refs[2 * pairs :]
        added_refs = refs[:2] if added is not None else None
        out_refs = refs[2 if added is not None else 0 :]
        for h in range(2):

            @pl.when(pl.program_id(0) // per == h)
            def _():
                chosen = [
                    jnp.concatenate(
                        [left_ref[:, p * cut : (p + 1) * cut] for p in picks[h]], axis=1
                    )
                    for left_ref in left_refs
                ]
                term = dot_rows([(a, ref[...]) for a, ref in zip(chosen, right_refs)])
                if added_refs is not None:
                    term = term + added_refs[h][...].astype(f32)
                first = 0
                for i, (blocks, kind) in enumerate(kinds):
                    out_refs[2 * i + h][...] = term[first : first + blocks * cut].astype(kind)
                    first += blocks * cut

    def halves(blocks):
        return [
            pl.BlockSpec((blocks * cut, wide), lambda n: (0, jnp.minimum(n, per - 1))),
            pl.BlockSpec((blocks * cut, wide), lambda n: (0, jnp.maximum(n - per, 0))),
        ]

    return pl.pallas_call(
        kernel,
        grid=(2 * per,),
        in_specs=[pl.BlockSpec((depth, columns), lambda n: (0, 0))] * pairs
        + [pl.BlockSpec((depth, wide), lambda n: (0, n))] * pairs
        + (halves(count) if added is not None else []),
        out_specs=[spec for blocks, _ in kinds for spec in halves(blocks)],
        out_shape=[
            jax.ShapeDtypeStruct((blocks * cut, half), kind)
            for blocks, kind in kinds
            for _ in range(2)
        ],
        compiler_params=pltpu.CompilerParams(vmem_limit_bytes=40 * 2**20),
        cost_estimate=pl.CostEstimate(flops=0, bytes_accessed=0, transcendentals=0),
    )(*lefts, *rights, *(added if added is not None else ()))


def lay_out(ups, downs, cut, order):
    planes, chips = lax.axis_size("tp"), len(order)
    rows, piece = ups[0].shape
    me = lax.axis_index("seq")
    where = jnp.stack([lax.axis_index("tp"), me >> 1, me & 1]).astype(jnp.int32)

    def kernel(where_ref, *refs):
        parts, (whole_ref, mine_ref, theirs_ref, whole, in_sem, out_sem) = refs[:-6], refs[-6:]
        plane, chip, core = where_ref[0], where_ref[1], where_ref[2]

        def place(part, b):
            return pltpu.make_async_copy(part, whole.at[:, b * piece : (b + 1) * piece], in_sem)

        for at, part in enumerate(parts):
            for b in range(planes):
                if 0 <= b - at + planes - 1 < planes:

                    @pl.when(plane == b - at + planes - 1)
                    def _():
                        place(part, b).start()

        for b in range(planes):
            place(parts[0], b).wait()
        copies = [pltpu.make_async_copy(whole, whole_ref, out_sem.at[0])]
        for at, mask in enumerate(order):
            for which, ref in ((core, mine_ref), (1 - core, theirs_ref)):
                column = pl.multiple_of(((chip ^ mask) * 2 + which) * cut, LANES)
                copies.append(
                    pltpu.make_async_copy(
                        whole.at[:, pl.ds(column, cut)],
                        ref.at[:, at * cut : (at + 1) * cut],
                        out_sem.at[len(copies)],
                    )
                )
        for copy in copies:
            copy.start()
        for copy in copies:
            copy.wait()

    parts = ups[:0:-1] + downs
    anywhere = pl.BlockSpec(memory_space=pl.ANY)
    return pl.pallas_call(
        kernel,
        in_specs=[pl.BlockSpec(memory_space=pltpu.SMEM)] + [anywhere] * len(parts),
        out_specs=[anywhere] * 3,
        out_shape=[
            jax.ShapeDtypeStruct((rows, planes * piece), bf16),
            jax.ShapeDtypeStruct((rows, chips * cut), bf16),
            jax.ShapeDtypeStruct((rows, chips * cut), bf16),
        ],
        scratch_shapes=[
            pltpu.VMEM((rows, planes * piece), bf16),
            pltpu.SemaphoreType.DMA,
            pltpu.SemaphoreType.DMA((1 + 2 * chips,)),
        ],
        compiler_params=pltpu.CompilerParams(vmem_limit_bytes=16 * 2**20),
        cost_estimate=pl.CostEstimate(flops=0, bytes_accessed=0, transcendentals=0),
    )(where, *parts)


def local(
    hidden,
    cotangent,
    router_gate,
    recursion_depth,
    live_counts,
    out_weight,
    adapter_down,
    adapter_up,
):
    shards, planes = lax.axis_size("seq"), lax.axis_size("tp")
    me, plane = lax.axis_index("seq"), lax.axis_index("tp")
    core, chip = me & 1, me >> 1
    chips = shards // 2
    chip_bits = list(range(1, shards.bit_length() - 1))
    rows, width = hidden.shape
    own_outs = width * planes // shards
    per_block = width // own_outs
    rank_rows = adapter_up.shape[0]
    rank = rank_rows * shards // NREC
    half = width // 2
    order = [i ^ (i >> 1) for i in range(chips)]
    cuts, first = [], 0
    for share in chunk_sizes(own_outs // LANES):
        cuts.append((first, share * LANES))
        first += share * LANES

    live = jnp.arange(rows, dtype=jnp.int32) < lax.dynamic_index_in_dim(live_counts, me, 0, False)
    dy = jnp.where(live[:, None], cotangent, jnp.zeros((), bf16))
    gate, depth = router_gate.astype(f32), recursion_depth.astype(f32)
    state = {"whole": {}, "step": 0, "hold": False, "weight": jnp.zeros((own_outs, width), f32)}

    pieces = [
        jnp.concatenate(
            [dy[:, i * own_outs + start : i * own_outs + start + cut] for i in range(per_block)],
            axis=1,
        )
        for start, cut in cuts
    ]

    def line():
        later = pieces
        for j in range(len(cuts)):
            ups, downs = [later[0]], [later[0]]
            later = later[1:]
            for k in range(1, planes):
                if state["hold"]:
                    state["hold"] = False
                    later = yield later
                state["step"] = k
                up = lax.ppermute(ups[-1], "tp", [(i, i + 1) for i in range(k - 1, planes - 1)])
                down = lax.ppermute(downs[-1], "tp", [(i, i - 1) for i in range(1, planes - k + 1)])
                up, down, later = yield (up, down, later)
                ups.append(up)
                downs.append(down)
            state["whole"][j] = (ups, downs)
        state["step"] = 0

    def columns(values, size, wanted):
        spots = [order.index(m) for m in wanted]
        lo, hi = min(spots), max(spots)
        if hi - lo + 1 == len(spots):
            return values[:, lo * size : (hi + 1) * size], [order[i] for i in range(lo, hi + 1)]
        return jnp.concatenate([values[:, i * size : (i + 1) * size] for i in spots], axis=1), wanted

    def scatter(jobs, size):
        sums, sent = [], []
        for pairs, bits in jobs:
            first_bit = bits[0] - 1
            away = [m for m in range(chips) if m >> first_bit & 1]
            away_pairs = [(columns(a, size, away)[0], b) for a, b in pairs]
            sent.append((dot_rows(away_pairs).astype(bf16), columns(pairs[0][0], size, away)[1]))
            sums.append({})
        made = yield [values for values, _ in sent]
        while state["step"] > 1:
            made = yield made
        made = yield [flip(values, bits[0]) for values, (_, bits) in zip(made, jobs)]
        for step in range(1, len(chip_bits) + 1):
            sent_before, sent = sent, []
            for total, got, (_, at), (pairs, bits) in zip(sums, made, sent_before, jobs):
                before = 1 << (bits[step - 1] - 1)
                arrived = {
                    m ^ before: got[i * size : (i + 1) * size].astype(f32) for i, m in enumerate(at)
                }
                for m in arrived:
                    own = total.pop(m, None)
                    if own is None:
                        own = dot_rows([(columns(a, size, [m])[0], b) for a, b in pairs])
                    total[m] = own + arrived[m]
                if step < len(chip_bits):
                    moving = [m for m in total if m >> (bits[step] - 1) & 1]
                    sent.append(([total.pop(m).astype(bf16) for m in moving], moving))
            if step < len(chip_bits):
                made = [jnp.concatenate(values, axis=0) for values, _ in sent]
                made, sums = yield (made, sums)
                while state["step"] > 1:
                    made = yield made
                made = yield [flip(values, bits[step]) for values, (_, bits) in zip(made, jobs)]
        return [total[0] for total in sums]

    def weights():
        small = jnp.stack([router_gate, recursion_depth.astype(bf16)])
        other_small, now = yield (flip(small, 0), hidden)
        other_hidden = flip(now, 0)
        gated = (gate[:, None] * hidden.astype(f32)).astype(bf16)
        other_hidden, gated, now = yield (other_hidden, gated, dy)
        other_dy = flip(now, 0)
        other_gate, other_depth = other_small[0].astype(f32), other_small[1].astype(f32)
        other_gated = (other_gate[:, None] * other_hidden.astype(f32)).astype(bf16)
        state["other"] = yield (other_hidden, other_dy, other_depth)
        state["gated"] = (gated, other_gated)

    def weight_chunk(j):
        start, cut = cuts[j]
        while j not in state["whole"]:
            yield ()
        whole, mine, theirs = lay_out(*state["whole"][j], cut, order)
        left = (mine, flip(theirs, 0))
        if j == 0:
            whole, left = yield (whole, left)
        state["terms"].append(whole)
        paths = [[bit - 1 for bit in chip_bits], [bit - 1 for bit in chip_bits[::-1]]]
        stay = []
        for bits in paths:
            kept = [m for m in range(chips) if not m >> bits[0] & 1]
            if len(bits) > 1:
                gone = [m for m in kept if m >> bits[1] & 1]
                kept = gone + [m ^ 1 << bits[1] for m in gone]
            stay.append(kept)
        away = [[m | 1 << bits[0] for m in kept] for kept, bits in zip(stay, paths)]
        spots = [[order.index(m) for m in kept] for kept in away]
        sent = column_products(left, state["gated"], cut, spots, len(spots[0]))
        sent, left = yield (sent, left)
        got = yield [flip(values, bits[0] + 1) for values, bits in zip(sent, paths)]
        spots = [[order.index(m) for m in kept] for kept in stay]
        parts = column_products(left, state["gated"], cut, spots, chips // 4, got)
        moved, rest = (parts[:2], parts[2:]) if len(parts) > 2 else (None, parts)
        for step in range(1, len(chip_bits)):
            got, rest = yield ([flip(values, bits[step] + 1) for values, bits in zip(moved, paths)], rest)
            rest = [own + new.astype(f32) for own, new in zip(rest, got)]
            stay = [kept[len(kept) // 2 :] for kept in stay]
            if step + 1 < len(chip_bits):
                moved, after = [], []
                for total, kept, bits in zip(rest, stay, paths):
                    place = {m: total[i * cut : (i + 1) * cut] for i, m in enumerate(kept)}
                    gone = [m for m in kept if m >> bits[step + 1] & 1]
                    moved.append(jnp.concatenate([place[m].astype(bf16) for m in gone], axis=0))
                    after.append([place[m ^ 1 << bits[step + 1]] for m in gone])
                    kept[:] = gone + [m ^ 1 << bits[step + 1] for m in gone]
                rest = [jnp.concatenate(values, axis=0) for values in after]
        state["weight"] = lax.dynamic_update_slice(
            state["weight"], jnp.concatenate(rest, axis=1), (start, 0)
        )

    state["terms"] = []

    def rows_of_pre():
        weight_blocks = out_weight.reshape(shards, own_outs, width)

        def term(j):
            return (state["terms"][j], weight_blocks, *cuts[j])

        total = None
        for j in range(len(cuts) - 1):
            while len(state["terms"]) <= j:
                yield ()
            state["terms"][j] = yield state["terms"][j]
            (total,) = yield add_products(total, [term(j)])
        while len(state["terms"]) < len(cuts) or "adapter_terms" not in state:
            yield ()
        total, state["terms"][-1] = yield (total, state["terms"][-1])
        late = [term(len(cuts) - 1)] + state["adapter_terms"]
        hidden_grad, gate_part = yield add_products(total, late, (gate, hidden))
        state["rows"] = (hidden_grad, lax.psum(gate_part[:, 0], "tp"))

    def adapters():
        parts = [adapter_down.T[None], adapter_up[None]]
        paths = [chip_bits, chip_bits[::-1]]
        for step in range(len(chip_bits)):
            got = yield [flip(part, bits[step]) for part, bits in zip(parts, paths)]
            parts = [jnp.concatenate(two, axis=0) for two in zip(parts, got)]
        splits = rank // rank_rows

        def wide(values, part):
            return lax.dot_general(
                values, part.reshape(-1, width), contract_last, preferred_element_type=f32
            )

        sources = (hidden, dy)
        got, first = yield (
            [flip(part, 0) for part in parts],
            [wide(values, part) for values, part in zip(sources, parts)],
        )
        blocks, products = [], []
        for values, part, other, product, bits in zip(sources, parts, got, first, paths):
            masks = masks_of(bits)
            blocks.append([(part, masks), (other, [m ^ 1 for m in masks])])
            products.append([(product, masks), (wide(values, other), [m ^ 1 for m in masks])])

        def select(products):
            out = [0.0] * splits
            for product, masks in products:
                for i, mask in enumerate(masks):
                    device = me ^ mask
                    here = depth == (device // splits + 1).astype(f32)
                    block = product[:, i * rank_rows : (i + 1) * rank_rows]
                    for h in range(splits):
                        out[h] += jnp.where((here & (device % splits == h))[:, None], block, 0.0)
            return out

        part = jnp.concatenate(select(products[0]) + select(products[1]), axis=1)
        part, blocks = yield (part, blocks[0])
        below = above = jnp.zeros_like(part)
        while state["step"] not in (0, min(2, planes - 1)):
            part = yield part
        for k in range(1, planes):
            sent = part + jnp.where(plane == k - 1, below, above)
            got = lax.ppermute(
                sent.astype(bf16), "tp", [(k - 1, k), (planes - k, planes - k - 1)]
            )
            if k == planes - 2 and state["step"]:
                state["hold"] = True
            got = yield got
            below = below + jnp.where(plane == k, got.astype(f32), 0.0)
            above = above + jnp.where(plane == planes - k - 1, got.astype(f32), 0.0)
        summed = part + below + above
        down, up = summed[:, :rank], adapter_scale * summed[:, rank:]

        def spread(masks):
            out = []
            for mask in masks:
                device = me ^ mask
                here = depth == (device // splits + 1).astype(f32)
                block = lax.dynamic_slice_in_dim(up, device % splits * rank_rows, rank_rows, axis=1)
                out.append(jnp.where(here[:, None], block, 0.0).astype(bf16))
            return jnp.concatenate(out, axis=1)

        state["adapter_terms"] = [
            (spread(masks), gathered, 0, rank_rows) for gathered, masks in blocks
        ]
        grads = jnp.concatenate(
            [gate[:, None] * up, gate[:, None] * adapter_scale * down], axis=1
        ).astype(bf16)
        grads, other_grads = yield (grads, flip(grads, 0))
        other_hidden, other_dy, other_depth = state["other"]

        def rank_columns(values, depths):
            parts = []
            for m in order:
                start = ((chip ^ m) * 2 + core) * rank_rows
                part = lax.dynamic_slice_in_dim(values, start % rank, rank_rows, axis=1)
                here = depths == (start // rank + 1).astype(f32)
                parts.append(jnp.where(here[:, None], part, jnp.zeros((), bf16)))
            return jnp.concatenate(parts, axis=1)

        jobs = []
        for at, own, other, bits in (
            (0, hidden, other_hidden, chip_bits),
            (rank, dy, other_dy, chip_bits[::-1]),
        ):
            pairs = [
                (rank_columns(grads[:, at : at + rank], depth), own),
                (rank_columns(other_grads[:, at : at + rank], other_depth), other),
            ]
            jobs.append((pairs, bits))
        state["adapter_grads"] = yield from scatter(jobs, rank_rows)

    count = range(len(cuts))
    run(
        [line(), weights(), adapters()]
        + [weight_chunk(j) for j in range(len(cuts))]
        + [rows_of_pre()]
    )
    hidden_grad, gate_grad = state["rows"]
    down_grad, up_grad = state["adapter_grads"]
    return (hidden_grad, gate_grad, state["weight"], down_grad, up_grad)


def solution(mesh):
    in_specs = (
        P("seq", "tp"),
        P("seq", "tp"),
        P("seq"),
        P("seq"),
        P(),
        P(None, "tp"),
        P("tp", "seq"),
        P("seq", "tp"),
    )
    out_specs = (P("seq", "tp"), P("seq"), P("seq", "tp"), P("seq", "tp"), P("seq", "tp"))
    return jax.shard_map(local, mesh=mesh, in_specs=in_specs, out_specs=out_specs, check_vma=False)
```

time: 573 us -> 477 us (0.83)
  Pallas kernels: 0 us -> 113 us
  matrix products: 125 us -> 46.8 us
  other arithmetic: 110 us -> 54.8 us
  local copies, waits for them, and re-layouts: 78.3 us -> 41.4 us
  waiting for transfers between devices: 148 us -> 115 us
  starting transfers between devices: 87.3 us -> 80.3 us
    pallas_call x0 -> x16, Pallas kernels: none -> 113 us  [the longest x4 50.5 us: add_products(): pl.pallas_call(kernel, grid=(tiles,), in_specs=in_specs, out_specs=out_sp...]
    dot_general x27 -> x16, matrix products: 125 us -> 46.8 us  [the longest x12 30.9 us: dot_rows(): lax.dot_general(a, b, contract_rows, preferred_element_type=f32)]
    concatenate x18 -> x12, other arithmetic: 69.3 us -> 15.4 us  [the longest x4 4.87 us: adapters(): parts = [jnp.concatenate(two, axis=0) for two in zip(parts, got)]]
    slice x7 -> x3, local copies, waits for them, and re-layouts: 25.5 us -> 5.82 us  [the longest x1 3.21 us: local(): dy[:, i * own_outs + start:i * own_outs + start + cut]]
    ppermute x30 -> x27, waiting for transfers between devices: 103 us -> 84.2 us  [the longest x12 76.6 us: line(): lax.ppermute(downs[-1], 'tp', [(i, i - 1) for i in range(1, planes - k +...]
    ppermute x34, waiting for transfers between devices: 44.7 us -> 30.5 us  [flip(): return lax.ppermute(value, 'seq', [(i, i ^ 1 << bit) for i in range(size)])]
    gather x4 -> x0, local copies, waits for them, and re-layouts: 11.4 us -> none  [the longest x2 10.1 us: gather_seq(): have = jnp.take(have, order, axis=0, mode='clip')]
    ppermute x30 -> x27, starting transfers between devices: 60.9 us -> 54.6 us  [the longest x12 33 us: line(): lax.ppermute(ups[-1], 'tp', [(i, i + 1) for i in range(k - 1, planes - 1)])]
  transfers between devices with their start and end apart: 64 -> 61, of which waited for: 17 -> 20; matrix products, arithmetic and copies ran while one was open for 53% -> 20% of each run, Pallas kernels for 0% -> 19%
where the time goes in v2:
time: 477 us; the launch traced here: 469 us
  waiting for transfers between devices  115 us (24%)
  Pallas kernels  113 us (24%)
  starting transfers between devices  80.3 us (17%)
  other arithmetic  54.8 us (11%)
  matrix products  46.8 us (10%)
  local copies, waits for them, and re-layouts  41.4 us (9%)
  blocking collectives  14.4 us (3%)
    ppermute x12, waiting for transfers between devices, line(): lax.ppermute(downs[-1], 'tp', [(i, i - 1) for i in range(1, planes - k +...  76.6 us
    pallas_call x4, Pallas kernels, add_products(): pl.pallas_call(kernel, grid=(tiles,), in_specs=in_specs, out_specs=out_sp...  50.5 us
    pallas_call x8, Pallas kernels, column_products(): pl.pallas_call(kernel, grid=(2 * per,), in_specs=[pl.BlockSpec((depth, co...  50 us
    unnamed x237, local copies, waits for them, and re-layouts  34.1 us
    ppermute x12, starting transfers between devices, line(): lax.ppermute(ups[-1], 'tp', [(i, i + 1) for i in range(k - 1, planes - 1)])  33 us
    dot_general x12, matrix products, dot_rows(): lax.dot_general(a, b, contract_rows, preferred_element_type=f32)  30.9 us
    ppermute x34, waiting for transfers between devices, flip(): return lax.ppermute(value, 'seq', [(i, i ^ 1 << bit) for i in range(size)])  30.5 us
    ppermute x34, starting transfers between devices, flip(): return lax.ppermute(value, 'seq', [(i, i ^ 1 << bit) for i in range(size)])  25.6 us
  transfers between devices with their start and end apart: 61, of which 20 were waited for; matrix products, arithmetic and copies ran while one was open for 20% of the time, Pallas kernels for 19%

profile of v2, /device:TPU:0, one launch (start us, length us, event | category | flops | bytes accessed | tf_op | source)
XLA Modules:
  0.0 468.6 jit_solution(16671595057133828305)
XLA Ops:
  11.1 6.5 %collective-permute-start = (bf16[768,512]{1,0:T(8,128)(2,1)S(1)}, bf16[768,512]{1,0:T(8,128)(2,1)}, u32[]{:S(2)}, u32[]{:S(2)}) collective-permute-start(bf16[768,512]{1,0:T(8,128)(2,1)S(1)} %pad_maximum_fusion.5.refs_3_), channel_id=1, source_target_pairs={{0,1},{1,2},{2,3},{4,5},{5,6},{6,7},{8,9},{9,10},{10,11},{12,13},{... | collective-permute-start | bytes 2359304 | tf_op jit(solution)/shard_map/ppermute | solution.py:288
  26.3 5.0 %collective-permute-done.3 = bf16[1,128,2048]{2,1,0:T(8,128)(2,1)S(1)} collective-permute-done((bf16[1,128,2048]{2,1,0:T(8,128)(2,1)S(1)}, bf16[1,128,2048]{2,1,0:T(8,128)(2,1)S(1)}, u32[]{:S(2)}, u32[]{:S(2)}) %collective-permute-start.3) | collective-permute-done | bytes 524320 | tf_op jit(solution)/shard_map/ppermute | solution.py:25
  40.3 23.1 %collective-permute-done.6.refs_5_ = bf16[768,512]{1,0:T(8,128)(2,1)} collective-permute-done((bf16[768,512]{1,0:T(8,128)(2,1)}, bf16[768,512]{1,0:T(8,128)(2,1)}, u32[]{:S(2)}, u32[]{:S(2)}) %collective-permute-start.6) | collective-permute-done | bytes 786464 | tf_op jit(solution)/shard_map/ppermute | solution.py:289
  73.8 4.5 fusion.91
  81.9 12.7 %collective-permute-done.11.refs_6_ = bf16[768,512]{1,0:T(8,128)(2,1)S(1)} collective-permute-done((bf16[768,512]{1,0:T(8,128)(2,1)}, bf16[768,512]{1,0:T(8,128)(2,1)S(1)}, u32[]{:S(2)}, u32[]{:S(2)}) %collective-permute-start.11) | collective-permute-done | bytes 786464 | tf_op jit(solution)/shard_map/ppermute | solution.py:289
  95.9 5.5 %collective-permute-start.15 = (bf16[768,512]{1,0:T(8,128)(2,1)S(1)}, bf16[768,512]{1,0:T(8,128)(2,1)}, u32[]{:S(2)}, u32[]{:S(2)}) collective-permute-start(bf16[768,512]{1,0:T(8,128)(2,1)S(1)} %copy-done.24), channel_id=1, source_target_pairs={{0,1},{1,2},{2,3},{4,5},{5,6},{6,7},{8,9},{9,10},{10,11},{12,13},{... | collective-permute-start | bytes 2359304 | tf_op jit(solution)/shard_map/ppermute | solution.py:288
  101.4 4.4 fusion.92
  130.1 5.0 %shard_map.120 = (bf16[512,1024]{1,0:T(8,128)(2,1)S(1)}, bf16[512,1024]{1,0:T(8,128)(2,1)S(1)}) custom-call(bf16[768,1024]{1,0:T(8,128)(2,1)S(1)} %copy-done.11, bf16[768,1024]{1,0:T(8,128)(2,1)S(1)} %copy-done.13, bf16[768,2048]{1,0:T(8,128)(2,1)S(1)} %multiply_convert_fusion.1.refs_2_, bf16[768,2048]{1,0:T(8,128)(2,1)S(1)} %multiply_convert_fusion.refs_3_), custom_call_target="tpu_custom_call" | custom-call | tf_op jit(solution)/shard_map/pallas_call | solution.py:161
  135.1 5.7 %collective-permute-done.20 = bf16[768,512]{1,0:T(8,128)(2,1)} collective-permute-done((bf16[768,512]{1,0:T(8,128)(2,1)}, bf16[768,512]{1,0:T(8,128)(2,1)}, u32[]{:S(2)}, u32[]{:S(2)}) %collective-permute-start.20) | collective-permute-done | bytes 786464 | tf_op jit(solution)/shard_map/ppermute | solution.py:455
  140.8 6.6 %collective-permute-done.19.refs_5_ = bf16[768,512]{1,0:T(8,128)(2,1)} collective-permute-done((bf16[768,512]{1,0:T(8,128)(2,1)}, bf16[768,512]{1,0:T(8,128)(2,1)}, u32[]{:S(2)}, u32[]{:S(2)}) %collective-permute-start.19) | collective-permute-done | bytes 786464 | tf_op jit(solution)/shard_map/ppermute | solution.py:289
  154.4 10.6 %shard_map.121.refs_0_ = f32[768,2048]{1,0:T(8,128)} custom-call(bf16[768,2048]{1,0:T(8,128)(2,1)S(1)} %copy-done.27, bf16[8,1024,2048]{2,1,0:T(8,128)(2,1)} %bitcast.37), custom_call_target="tpu_custom_call" | custom-call | tf_op jit(solution)/shard_map/pallas_call | solution.py:105
  165.0 8.3 %collective-permute-done.22.refs_6_ = bf16[768,512]{1,0:T(8,128)(2,1)S(1)} collective-permute-done((bf16[768,512]{1,0:T(8,128)(2,1)}, bf16[768,512]{1,0:T(8,128)(2,1)S(1)}, u32[]{:S(2)}, u32[]{:S(2)}) %collective-permute-start.22) | collective-permute-done | bytes 786464 | tf_op jit(solution)/shard_map/ppermute | solution.py:289
  183.9 6.6 %shard_map.122 = (bf16[256,1024]{1,0:T(8,128)(2,1)}, bf16[256,1024]{1,0:T(8,128)(2,1)}, f32[256,1024]{1,0:T(8,128)S(1)}, f32[256,1024]{1,0:T(8,128)S(1)}) custom-call(bf16[768,1024]{1,0:T(8,128)(2,1)S(1)} %copy-done.11, bf16[768,1024]{1,0:T(8,128)(2,1)S(1)} %copy-done.13, bf16[768,2048]{1,0:T(8,128)(2,1)S(1)} %multiply_convert_fusion.1.refs_2_, ...), custom_call_target="tpu_custom_call" | custom-call | tf_op jit(solution)/shard_map/pallas_call | solution.py:161
  196.3 7.1 %collective-permute-start.26 = (bf16[768,512]{1,0:T(8,128)(2,1)}, bf16[768,512]{1,0:T(8,128)(2,1)}, u32[]{:S(2)}, u32[]{:S(2)}) collective-permute-start(bf16[768,512]{1,0:T(8,128)(2,1)} %get-tuple-element.234.refs_3_), channel_id=1, source_target_pairs={{0,1},{1,2},{2,3},{4,5},{5,6},{6,7},{8,9},{9,10},{10,11},{12,13},{... | collective-permute-start | bytes 2359304 | tf_op jit(solution)/shard_map/ppermute | solution.py:288
  206.7 7.2 %shard_map.124 = (bf16[512,1024]{1,0:T(8,128)(2,1)}, bf16[512,1024]{1,0:T(8,128)(2,1)}) custom-call(bf16[768,1024]{1,0:T(8,128)(2,1)S(1)} %copy-done.5, bf16[768,1024]{1,0:T(8,128)(2,1)} %collective-permute-done.31.refs_1_, bf16[768,2048]{1,0:T(8,128)(2,1)S(1)} %multiply_convert_fusion.1.refs_2_, bf16[768,2048]{1,0:T(8,128)(2,1)S(1)} %copy-done.1), custom_call_target="tpu_custom_call" | custom-call | tf_op jit(solution)/shard_map/pallas_call | solution.py:161
  223.3 11.7 %shard_map.125.refs_0_ = f32[768,2048]{1,0:T(8,128)} custom-call(f32[768,2048]{1,0:T(8,128)} %shard_map.121.refs_0_, bf16[768,2048]{1,0:T(8,128)(2,1)S(1)} %copy-done.15, bf16[8,1024,2048]{2,1,0:T(8,128)(2,1)} %bitcast.38), custom_call_target="tpu_custom_call", output_to_operand_aliasing={{}: (0, {})} | custom-call | tf_op jit(solution)/shard_map/pallas_call | solution.py:105
  239.2 6.9 %shard_map.126 = (bf16[256,1024]{1,0:T(8,128)(2,1)S(1)}, bf16[256,1024]{1,0:T(8,128)(2,1)S(1)}, f32[256,1024]{1,0:T(8,128)S(1)}, f32[256,1024]{1,0:T(8,128)S(1)}) custom-call(bf16[768,1024]{1,0:T(8,128)(2,1)S(1)} %copy-done.6, bf16[768,1024]{1,0:T(8,128)(2,1)} %collective-permute-done.31.refs_1_, bf16[768,2048]{1,0:T(8,128)(2,1)S(1)} %multiply_convert_fusion.1.refs_2_, ...), custom_call_target="tpu_custom_call" | custom-call | tf_op jit(solution)/shard_map/pallas_call | solution.py:161
  257.3 4.0 fusion.1
  265.2 7.2 %collective-permute-done.36.refs_5_ = bf16[768,512]{1,0:T(8,128)(2,1)S(1)} collective-permute-done((bf16[768,512]{1,0:T(8,128)(2,1)}, bf16[768,512]{1,0:T(8,128)(2,1)S(1)}, u32[]{:S(2)}, u32[]{:S(2)}) %collective-permute-start.36) | collective-permute-done | bytes 786464 | tf_op jit(solution)/shard_map/ppermute | solution.py:289
  274.6 16.4 %collective-permute-done.40.refs_6_ = bf16[768,512]{1,0:T(8,128)(2,1)S(1)} collective-permute-done((bf16[768,512]{1,0:T(8,128)(2,1)S(1)}, bf16[768,512]{1,0:T(8,128)(2,1)S(1)}, u32[]{:S(2)}, u32[]{:S(2)}) %collective-permute-start.40) | collective-permute-done | bytes 786464 | tf_op jit(solution)/shard_map/ppermute | solution.py:289
  302.7 4.6 collective-permute-start.41
  314.3 6.2 %shard_map.128 = (bf16[512,1024]{1,0:T(8,128)(2,1)S(1)}, bf16[512,1024]{1,0:T(8,128)(2,1)S(1)}) custom-call(bf16[768,1024]{1,0:T(8,128)(2,1)S(1)} %copy-done.8, bf16[768,1024]{1,0:T(8,128)(2,1)} %collective-permute-done.45.refs_1_, bf16[768,2048]{1,0:T(8,128)(2,1)S(1)} %multiply_convert_fusion.1.refs_2_, bf16[768,2048]{1,0:T(8,128)(2,1)S(1)} %copy-done.2), custom_call_target="tpu_custom_call" | custom-call | tf_op jit(solution)/shard_map/pallas_call | solution.py:161
  336.3 11.6 %shard_map.129.refs_0_ = f32[768,2048]{1,0:T(8,128)} custom-call(f32[768,2048]{1,0:T(8,128)} %shard_map.125.refs_0_, bf16[768,2048]{1,0:T(8,128)(2,1)S(1)} %copy-done.17, bf16[8,1024,2048]{2,1,0:T(8,128)(2,1)} %bitcast.39), custom_call_target="tpu_custom_call", output_to_operand_aliasing={{}: (0, {})} | custom-call | tf_op jit(solution)/shard_map/pallas_call | solution.py:105
  347.9 4.2 fusion.2
  363.9 6.5 %shard_map.130 = (bf16[256,1024]{1,0:T(8,128)(2,1)S(1)}, bf16[256,1024]{1,0:T(8,128)(2,1)S(1)}, f32[256,1024]{1,0:T(8,128)S(1)}, f32[256,1024]{1,0:T(8,128)S(1)}) custom-call(bf16[768,1024]{1,0:T(8,128)(2,1)S(1)} %copy-done.9, bf16[768,1024]{1,0:T(8,128)(2,1)} %collective-permute-done.45.refs_1_, bf16[768,2048]{1,0:T(8,128)(2,1)S(1)} %multiply_convert_fusion.1.refs_2_, ...), custom_call_target="tpu_custom_call" | custom-call | tf_op jit(solution)/shard_map/pallas_call | solution.py:161
  373.3 9.2 %collective-permute-done.52 = bf16[256,1024]{1,0:T(8,128)(2,1)S(1)} collective-permute-done((bf16[256,1024]{1,0:T(8,128)(2,1)S(1)}, bf16[256,1024]{1,0:T(8,128)(2,1)S(1)}, u32[]{:S(2)}, u32[]{:S(2)}) %collective-permute-start.52) | collective-permute-done | bytes 524320 | tf_op jit(solution)/shard_map/ppermute | solution.py:25
  391.4 4.4 select_maximum_fusion
  398.2 5.0 %shard_map.132 = (bf16[512,1024]{1,0:T(8,128)(2,1)S(1)}, bf16[512,1024]{1,0:T(8,128)(2,1)S(1)}) custom-call(bf16[768,1024]{1,0:T(8,128)(2,1)S(1)} %get-tuple-element.349.refs_0_, bf16[768,1024]{1,0:T(8,128)(2,1)S(1)} %collective-permute-done.56.refs_1_, bf16[768,2048]{1,0:T(8,128)(2,1)S(1)} %multiply_convert_fusion.1.refs_2_, bf16[768,2048]{1,0:T(8,128)(2,1)S(1)} %copy-done.3), custom_call_target="tpu_custom_call" | custom-call | tf_op jit(solution)/shard_map/pallas_call | solution.py:161
  403.2 6.8 %collective-permute-done.54 = bf16[128,2048]{1,0:T(8,128)(2,1)S(1)} collective-permute-done((bf16[128,2048]{1,0:T(8,128)(2,1)S(1)}, bf16[128,2048]{1,0:T(8,128)(2,1)S(1)}, u32[]{:S(2)}, u32[]{:S(2)}) %collective-permute-start.54) | collective-permute-done | bytes 524320 | tf_op jit(solution)/shard_map/ppermute | solution.py:25
  417.6 16.7 %shard_map.133 = (f32[768,2048]{1,0:T(8,128)}, f32[768,1]{1,0:T(8,128)S(1)}) custom-call(f32[768,2048]{1,0:T(8,128)} %shard_map.129.refs_0_, bf16[768,2048]{1,0:T(8,128)(2,1)} %copy-done.18, bf16[8,1024,2048]{2,1,0:T(8,128)(2,1)} %bitcast.40, bf16[768,512]{1,0:T(8,128)(2,1)S(1)} %pad_maximum_fusion.10.refs_3_, ...), custom_call_target="tpu_custom_call", output_to_operand_aliasing={{0}: (0, {})} | custom-call | tf_op jit(solution)/shard_map/pallas_call | solution.py:105
  436.6 6.7 %shard_map.134 = (bf16[256,1024]{1,0:T(8,128)(2,1)}, bf16[256,1024]{1,0:T(8,128)(2,1)}, f32[256,1024]{1,0:T(8,128)S(1)}, f32[256,1024]{1,0:T(8,128)S(1)}) custom-call(bf16[768,1024]{1,0:T(8,128)(2,1)S(1)} %get-tuple-element.349.refs_0_, bf16[768,1024]{1,0:T(8,128)(2,1)S(1)} %collective-permute-done.56.refs_1_, ...), custom_call_target="tpu_custom_call" | custom-call | tf_op jit(solution)/shard_map/pallas_call | solution.py:161
  448.8 14.4 %psum.7 = f32[768]{0:T(1024)} all-reduce(f32[768]{0:T(1024)S(1)} %reduce.2), channel_id=1, replica_groups=mesh['seq'=8,'tp'=4] {'tp'}, use_global_device_ids=true, to_apply=%region_0.1 | all-reduce | flops 768 | bytes 6144 | tf_op jit(solution)/shard_map/psum | solution.py:411
  (423 shorter events, 204.6 us)
Async XLA Ops:
  9.7 23.0 %collective-permute-start.1 = (bf16[768,512]{1,0:T(8,128)(2,1)S(1)}, bf16[768,512]{1,0:T(8,128)(2,1)}, u32[]{:S(2)}, u32[]{:S(2)}) collective-permute-start(bf16[768,512]{1,0:T(8,128)(2,1)S(1)} %pad_maximum_fusion.5.refs_3_), channel_id=1, source_target_pairs={{1,0},{2,1},{3,2},{5,4},{6,5},{7,6},{9,8},{10,9},{11,10},{13,12},{... | collective-permute-start | bytes 2359304 | tf_op jit(solution)/shard_map/ppermute | solution.py:289
  11.1 22.3 %collective-permute-start = (bf16[768,512]{1,0:T(8,128)(2,1)S(1)}, bf16[768,512]{1,0:T(8,128)(2,1)}, u32[]{:S(2)}, u32[]{:S(2)}) collective-permute-start(bf16[768,512]{1,0:T(8,128)(2,1)S(1)} %pad_maximum_fusion.5.refs_3_), channel_id=1, source_target_pairs={{0,1},{1,2},{2,3},{4,5},{5,6},{6,7},{8,9},{9,10},{10,11},{12,13},{... | collective-permute-start | bytes 2359304 | tf_op jit(solution)/shard_map/ppermute | solution.py:288
  33.4 30.0 %collective-permute-start.7 = (bf16[768,2048]{1,0:T(8,128)(2,1)S(1)}, bf16[768,2048]{1,0:T(8,128)(2,1)S(1)}, u32[]{:S(2)}, u32[]{:S(2)}) collective-permute-start(bf16[768,2048]{1,0:T(8,128)(2,1)S(1)} %copy-done.49), channel_id=1, source_target_pairs={{0,4},{4,0},{8,12},{12,8},{16,20},{20,16},{24,28},{28,24},{1,5},{5... | collective-permute-start | bytes 9437192 | tf_op jit(solution)/shard_map/ppermute | solution.py:25
  33.7 29.8 %collective-permute-start.9 = (bf16[2,128,2048]{2,1,0:T(8,128)(2,1)S(1)}, bf16[2,128,2048]{2,1,0:T(8,128)(2,1)S(1)}, u32[]{:S(2)}, u32[]{:S(2)}) collective-permute-start(bf16[2,128,2048]{2,1,0:T(8,128)(2,1)S(1)} %pad_maximum_fusion.4), channel_id=1, source_target_pairs={{0,8},{4,12},{8,0},{12,4},{16,24},{20,28},{24,16},{28,20},{1,9},{5... | collective-permute-start | bytes 3145736 | tf_op jit(solution)/shard_map/ppermute | solution.py:25
  35.4 28.0 %collective-permute-start.8 = (bf16[2,128,2048]{2,1,0:T(8,128)(2,1)S(1)}, bf16[2,128,2048]{2,1,0:T(8,128)(2,1)S(1)}, u32[]{:S(2)}, u32[]{:S(2)}) collective-permute-start(bf16[2,128,2048]{2,1,0:T(8,128)(2,1)S(1)} %pad_maximum_fusion.3), channel_id=1, source_target_pairs={{0,16},{4,20},{8,24},{12,28},{16,0},{20,4},{24,8},{28,12},{1,17},{... | collective-permute-start | bytes 3145736 | tf_op jit(solution)/shard_map/ppermute | solution.py:25
  38.5 25.0 %collective-permute-start.6 = (bf16[768,512]{1,0:T(8,128)(2,1)}, bf16[768,512]{1,0:T(8,128)(2,1)}, u32[]{:S(2)}, u32[]{:S(2)}) collective-permute-start(bf16[768,512]{1,0:T(8,128)(2,1)} %collective-permute-done.1.refs_4_), channel_id=1, source_target_pairs={{1,0},{2,1},{5,4},{6,5},{9,8},{10,9},{13,12},{14,13},{17,16},{18,1... | collective-permute-start | bytes 2359304 | tf_op jit(solution)/shard_map/ppermute | solution.py:289
  66.4 28.2 %collective-permute-start.12 = (bf16[768,2048]{1,0:T(8,128)(2,1)}, bf16[768,2048]{1,0:T(8,128)(2,1)}, u32[]{:S(2)}, u32[]{:S(2)}) collective-permute-start(bf16[768,2048]{1,0:T(8,128)(2,1)} %broadcast_select_fusion), channel_id=1, source_target_pairs={{0,4},{4,0},{8,12},{12,8},{16,20},{20,16},{24,28},{28,24},{1,5},{5... | collective-permute-start | bytes 9437192 | tf_op jit(solution)/shard_map/ppermute | solution.py:25
  69.6 25.0 %collective-permute-start.14 = (bf16[4,128,2048]{2,1,0:T(8,128)(2,1)}, bf16[4,128,2048]{2,1,0:T(8,128)(2,1)}, u32[]{:S(2)}, u32[]{:S(2)}) collective-permute-start(bf16[4,128,2048]{2,1,0:T(8,128)(2,1)} %pad_maximum_fusion.1), channel_id=1, source_target_pairs={{0,4},{4,0},{8,12},{12,8},{16,20},{20,16},{24,28},{28,24},{1,5},{5... | collective-permute-start | bytes 6291464 | tf_op jit(solution)/shard_map/ppermute | solution.py:25
  71.6 23.0 %collective-permute-start.13 = (bf16[4,128,2048]{2,1,0:T(8,128)(2,1)}, bf16[4,128,2048]{2,1,0:T(8,128)(2,1)}, u32[]{:S(2)}, u32[]{:S(2)}) collective-permute-start(bf16[4,128,2048]{2,1,0:T(8,128)(2,1)} %pad_maximum_fusion.refs_4_), channel_id=1, source_target_pairs={{0,4},{4,0},{8,12},{12,8},{16,20},{20,16},{24,28},{28,24},{1,5},{5... | collective-permute-start | bytes 6291464 | tf_op jit(solution)/shard_map/ppermute | solution.py:25
  72.5 22.0 %collective-permute-start.11 = (bf16[768,512]{1,0:T(8,128)(2,1)}, bf16[768,512]{1,0:T(8,128)(2,1)S(1)}, u32[]{:S(2)}, u32[]{:S(2)}) collective-permute-start(bf16[768,512]{1,0:T(8,128)(2,1)} %collective-permute-done.6.refs_5_), channel_id=1, source_target_pairs={{1,0},{5,4},{9,8},{13,12},{17,16},{21,20},{25,24},{29,28}} | collective-permute-start | bytes 2359304 | tf_op jit(solution)/shard_map/ppermute | solution.py:289
  94.6 24.2 %collective-permute-start.16 = (bf16[768,512]{1,0:T(8,128)(2,1)S(1)}, bf16[768,512]{1,0:T(8,128)(2,1)}, u32[]{:S(2)}, u32[]{:S(2)}) collective-permute-start(bf16[768,512]{1,0:T(8,128)(2,1)S(1)} %copy-done.24), channel_id=1, source_target_pairs={{1,0},{2,1},{3,2},{5,4},{6,5},{7,6},{9,8},{10,9},{11,10},{13,12},{... | collective-permute-start | bytes 2359304 | tf_op jit(solution)/shard_map/ppermute | solution.py:289
  95.9 22.9 %collective-permute-start.15 = (bf16[768,512]{1,0:T(8,128)(2,1)S(1)}, bf16[768,512]{1,0:T(8,128)(2,1)}, u32[]{:S(2)}, u32[]{:S(2)}) collective-permute-start(bf16[768,512]{1,0:T(8,128)(2,1)S(1)} %copy-done.24), channel_id=1, source_target_pairs={{0,1},{1,2},{2,3},{4,5},{5,6},{6,7},{8,9},{9,10},{10,11},{12,13},{... | collective-permute-start | bytes 2359304 | tf_op jit(solution)/shard_map/ppermute | solution.py:288
  126.0 21.4 %collective-permute-start.19 = (bf16[768,512]{1,0:T(8,128)(2,1)}, bf16[768,512]{1,0:T(8,128)(2,1)}, u32[]{:S(2)}, u32[]{:S(2)}) collective-permute-start(bf16[768,512]{1,0:T(8,128)(2,1)} %collective-permute-done.16.refs_4_), channel_id=1, source_target_pairs={{1,0},{2,1},{5,4},{6,5},{9,8},{10,9},{13,12},{14,13},{17,16},{18,1... | collective-permute-start | bytes 2359304 | tf_op jit(solution)/shard_map/ppermute | solution.py:289
  147.3 25.9 %collective-permute-start.24 = (bf16[512,1024]{1,0:T(8,128)(2,1)S(1)}, bf16[512,1024]{1,0:T(8,128)(2,1)S(1)}, u32[]{:S(2)}, u32[]{:S(2)}) collective-permute-start(bf16[512,1024]{1,0:T(8,128)(2,1)S(1)} %get-tuple-element.231), channel_id=1, source_target_pairs={{0,8},{4,12},{8,0},{12,4},{16,24},{20,28},{24,16},{28,20},{1,9},{5... | collective-permute-start | bytes 3145736 | tf_op jit(solution)/shard_map/ppermute | solution.py:25
  148.0 25.3 %collective-permute-start.25 = (bf16[512,1024]{1,0:T(8,128)(2,1)S(1)}, bf16[512,1024]{1,0:T(8,128)(2,1)S(1)}, u32[]{:S(2)}, u32[]{:S(2)}) collective-permute-start(bf16[512,1024]{1,0:T(8,128)(2,1)S(1)} %get-tuple-element.232), channel_id=1, source_target_pairs={{0,16},{4,20},{8,24},{12,28},{16,0},{20,4},{24,8},{28,12},{1,17},{... | collective-permute-start | bytes 3145736 | tf_op jit(solution)/shard_map/ppermute | solution.py:25
  182.6 31.3 %collective-permute-start.28 = (bf16[768,512]{1,0:T(8,128)(2,1)}, bf16[768,512]{1,0:T(8,128)(2,1)}, u32[]{:S(2)}, u32[]{:S(2)}) collective-permute-start(bf16[768,512]{1,0:T(8,128)(2,1)} %add_convert_fusion), channel_id=1, source_target_pairs={{2,3},{1,0},{6,7},{5,4},{10,11},{9,8},{14,15},{13,12},{18,19},{17,... | collective-permute-start | bytes 2359304 | tf_op jit(solution)/shard_map/ppermute | solution.py:455
  192.4 21.5 %collective-permute-start.29 = (bf16[256,1024]{1,0:T(8,128)(2,1)}, bf16[256,1024]{1,0:T(8,128)(2,1)}, u32[]{:S(2)}, u32[]{:S(2)}) collective-permute-start(bf16[256,1024]{1,0:T(8,128)(2,1)} %get-tuple-element.241), channel_id=1, source_target_pairs={{0,16},{4,20},{8,24},{12,28},{16,0},{20,4},{24,8},{28,12},{1,17},{... | collective-permute-start | bytes 1572872 | tf_op jit(solution)/shard_map/ppermute | solution.py:25
  195.0 40.0 %collective-permute-start.27 = (bf16[768,512]{1,0:T(8,128)(2,1)}, bf16[768,512]{1,0:T(8,128)(2,1)}, u32[]{:S(2)}, u32[]{:S(2)}) collective-permute-start(bf16[768,512]{1,0:T(8,128)(2,1)} %get-tuple-element.234.refs_3_), channel_id=1, source_target_pairs={{1,0},{2,1},{3,2},{5,4},{6,5},{7,6},{9,8},{10,9},{11,10},{13,12},{... | collective-permute-start | bytes 2359304 | tf_op jit(solution)/shard_map/ppermute | solution.py:289
  196.3 38.7 %collective-permute-start.26 = (bf16[768,512]{1,0:T(8,128)(2,1)}, bf16[768,512]{1,0:T(8,128)(2,1)}, u32[]{:S(2)}, u32[]{:S(2)}) collective-permute-start(bf16[768,512]{1,0:T(8,128)(2,1)} %get-tuple-element.234.refs_3_), channel_id=1, source_target_pairs={{0,1},{1,2},{2,3},{4,5},{5,6},{6,7},{8,9},{9,10},{10,11},{12,13},{... | collective-permute-start | bytes 2359304 | tf_op jit(solution)/shard_map/ppermute | solution.py:288
  213.9 24.8 %collective-permute-start.33 = (bf16[512,1024]{1,0:T(8,128)(2,1)}, bf16[512,1024]{1,0:T(8,128)(2,1)}, u32[]{:S(2)}, u32[]{:S(2)}) collective-permute-start(bf16[512,1024]{1,0:T(8,128)(2,1)} %get-tuple-element.254), channel_id=1, source_target_pairs={{0,8},{4,12},{8,0},{12,4},{16,24},{20,28},{24,16},{28,20},{1,9},{5... | collective-permute-start | bytes 3145736 | tf_op jit(solution)/shard_map/ppermute | solution.py:25
  214.7 24.5 %collective-permute-start.34 = (bf16[512,1024]{1,0:T(8,128)(2,1)}, bf16[512,1024]{1,0:T(8,128)(2,1)}, u32[]{:S(2)}, u32[]{:S(2)}) collective-permute-start(bf16[512,1024]{1,0:T(8,128)(2,1)} %get-tuple-element.255), channel_id=1, source_target_pairs={{0,16},{4,20},{8,24},{12,28},{16,0},{20,4},{24,8},{28,12},{1,17},{... | collective-permute-start | bytes 3145736 | tf_op jit(solution)/shard_map/ppermute | solution.py:25
  297.4 26.5 %collective-permute-start.43 = (bf16[256,2048]{1,0:T(8,128)(2,1)}, bf16[256,2048]{1,0:T(8,128)(2,1)S(1)}, u32[]{:S(2)}, u32[]{:S(2)}) collective-permute-start(bf16[256,2048]{1,0:T(8,128)(2,1)} %fusion), channel_id=1, source_target_pairs={{0,8},{4,12},{8,0},{12,4},{16,24},{20,28},{24,16},{28,20},{1,9},{5... | collective-permute-start | bytes 3145736 | tf_op jit(solution)/shard_map/ppermute | solution.py:25
  298.2 25.7 %collective-permute-start.44 = (bf16[256,2048]{1,0:T(8,128)(2,1)}, bf16[256,2048]{1,0:T(8,128)(2,1)S(1)}, u32[]{:S(2)}, u32[]{:S(2)}) collective-permute-start(bf16[256,2048]{1,0:T(8,128)(2,1)} %fusion.1), channel_id=1, source_target_pairs={{0,16},{4,20},{8,24},{12,28},{16,0},{20,4},{24,8},{28,12},{1,17},{... | collective-permute-start | bytes 3145736 | tf_op jit(solution)/shard_map/ppermute | solution.py:25
  301.4 21.3 %collective-permute-start.42 = (bf16[768,512]{1,0:T(8,128)(2,1)S(1)}, bf16[768,512]{1,0:T(8,128)(2,1)S(1)}, u32[]{:S(2)}, u32[]{:S(2)}) collective-permute-start(bf16[768,512]{1,0:T(8,128)(2,1)S(1)} %copy-done.19), channel_id=1, source_target_pairs={{1,0},{2,1},{3,2},{5,4},{6,5},{7,6},{9,8},{10,9},{11,10},{13,12},{... | collective-permute-start | bytes 2359304 | tf_op jit(solution)/shard_map/ppermute | solution.py:289
  324.0 29.9 %collective-permute-start.46 = (bf16[768,512]{1,0:T(8,128)(2,1)S(1)}, bf16[768,512]{1,0:T(8,128)(2,1)}, u32[]{:S(2)}, u32[]{:S(2)}) collective-permute-start(bf16[768,512]{1,0:T(8,128)(2,1)S(1)} %collective-permute-done.41.refs_2_), channel_id=1, source_target_pairs={{1,2},{2,3},{5,6},{6,7},{9,10},{10,11},{13,14},{14,15},{17,18},{18... | collective-permute-start | bytes 2359304 | tf_op jit(solution)/shard_map/ppermute | solution.py:288
  325.6 28.3 %collective-permute-start.47 = (bf16[768,512]{1,0:T(8,128)(2,1)S(1)}, bf16[768,512]{1,0:T(8,128)(2,1)}, u32[]{:S(2)}, u32[]{:S(2)}) collective-permute-start(bf16[768,512]{1,0:T(8,128)(2,1)S(1)} %collective-permute-done.42.refs_4_), channel_id=1, source_target_pairs={{1,0},{2,1},{5,4},{6,5},{9,8},{10,9},{13,12},{14,13},{17,16},{18,1... | collective-permute-start | bytes 2359304 | tf_op jit(solution)/shard_map/ppermute | solution.py:289
  327.2 26.7 %collective-permute-start.48 = (bf16[512,1024]{1,0:T(8,128)(2,1)S(1)}, bf16[512,1024]{1,0:T(8,128)(2,1)S(1)}, u32[]{:S(2)}, u32[]{:S(2)}) collective-permute-start(bf16[512,1024]{1,0:T(8,128)(2,1)S(1)} %get-tuple-element.293), channel_id=1, source_target_pairs={{0,8},{4,12},{8,0},{12,4},{16,24},{20,28},{24,16},{28,20},{1,9},{5... | collective-permute-start | bytes 3145736 | tf_op jit(solution)/shard_map/ppermute | solution.py:25
  328.6 26.3 %collective-permute-start.49 = (bf16[512,1024]{1,0:T(8,128)(2,1)S(1)}, bf16[512,1024]{1,0:T(8,128)(2,1)S(1)}, u32[]{:S(2)}, u32[]{:S(2)}) collective-permute-start(bf16[512,1024]{1,0:T(8,128)(2,1)S(1)} %get-tuple-element.294), channel_id=1, source_target_pairs={{0,16},{4,20},{8,24},{12,28},{16,0},{20,4},{24,8},{28,12},{1,17},{... | collective-permute-start | bytes 3145736 | tf_op jit(solution)/shard_map/ppermute | solution.py:25
  355.9 27.2 %collective-permute-start.50 = (bf16[768,512]{1,0:T(8,128)(2,1)}, bf16[768,512]{1,0:T(8,128)(2,1)}, u32[]{:S(2)}, u32[]{:S(2)}) collective-permute-start(bf16[768,512]{1,0:T(8,128)(2,1)} %collective-permute-done.46.refs_1_), channel_id=1, source_target_pairs={{2,3},{6,7},{10,11},{14,15},{18,19},{22,23},{26,27},{30,31}} | collective-permute-start | bytes 2359304 | tf_op jit(solution)/shard_map/ppermute | solution.py:288
  357.4 25.7 %collective-permute-start.51 = (bf16[768,512]{1,0:T(8,128)(2,1)}, bf16[768,512]{1,0:T(8,128)(2,1)}, u32[]{:S(2)}, u32[]{:S(2)}) collective-permute-start(bf16[768,512]{1,0:T(8,128)(2,1)} %collective-permute-done.47.refs_5_), channel_id=1, source_target_pairs={{1,0},{5,4},{9,8},{13,12},{17,16},{21,20},{25,24},{29,28}} | collective-permute-start | bytes 2359304 | tf_op jit(solution)/shard_map/ppermute | solution.py:289
  411.9 24.3 %collective-permute-start.57 = (bf16[512,1024]{1,0:T(8,128)(2,1)S(1)}, bf16[512,1024]{1,0:T(8,128)(2,1)S(1)}, u32[]{:S(2)}, u32[]{:S(2)}) collective-permute-start(bf16[512,1024]{1,0:T(8,128)(2,1)S(1)} %get-tuple-element.319), channel_id=1, source_target_pairs={{0,8},{4,12},{8,0},{12,4},{16,24},{20,28},{24,16},{28,20},{1,9},{5... | collective-permute-start | bytes 3145736 | tf_op jit(solution)/shard_map/ppermute | solution.py:25
  412.5 24.0 %collective-permute-start.58 = (bf16[512,1024]{1,0:T(8,128)(2,1)S(1)}, bf16[512,1024]{1,0:T(8,128)(2,1)S(1)}, u32[]{:S(2)}, u32[]{:S(2)}) collective-permute-start(bf16[512,1024]{1,0:T(8,128)(2,1)S(1)} %get-tuple-element.320), channel_id=1, source_target_pairs={{0,16},{4,20},{8,24},{12,28},{16,0},{20,4},{24,8},{28,12},{1,17},{... | collective-permute-start | bytes 3145736 | tf_op jit(solution)/shard_map/ppermute | solution.py:25
  (147 other events, 1324.5 us)
